TPU v7x, 32 devices: a whole 2x2x4 slice. The times are simulated.
32 devices in a mesh: dp: 8 (over z, x), seq: 4 (over y, core).
Axes of the slice: x: 2, y: 2, z: 4, core: 2. Of those that a mesh axis runs over, the one named last changes fastest.
Arguments:
- tokens_in: bfloat16 [2, 8, 1024, 512], P(None, 'dp', 'seq'), may hold values from -6 to 6
- grad_output: bfloat16 [2, 8, 1024, 512], P(None, 'dp', 'seq'), may hold values from -6 to 6
- prefix_len: int32 [2, 8], P(None, 'dp'), may hold values from 0 to 511
- w_qkv: bfloat16 [2, 512, 1536], P(None, ('dp', 'seq')), may hold values from -0.25 to 0.25
- w_out: bfloat16 [2, 512, 512], P(None, ('dp', 'seq')), may hold values from -0.75 to 0.75
- w_up: bfloat16 [2, 512, 2048], P(None, ('dp', 'seq')), may hold values from -0.25 to 0.25
- w_down: bfloat16 [2, 2048, 512], P(None, ('dp', 'seq')), may hold values from -0.125 to 0.125
- norm_gains: bfloat16 [2, 2, 512], P(None, None, ('dp', 'seq')), may hold values from 0.5 to 1.5
- bias_rows: bfloat16 [2, 6, 512], P(None, None, ('dp', 'seq')), may hold values from -1.5 to 1.5
- up_bias: bfloat16 [2, 2048], P(None, ('dp', 'seq')), may hold values from -1.5 to 1.5
Outputs:
- out_act: bfloat16 [2, 8, 1024, 512], P(None, 'dp', 'seq')
- grad_in: float32 [2, 8, 1024, 512], P(None, 'dp', 'seq')
- grad_qkv: float32 [2, 512, 1536], P(None, ('dp', 'seq'))
- grad_wout: float32 [2, 512, 512], P(None, ('dp', 'seq'))
- grad_wup: float32 [2, 512, 2048], P(None, ('dp', 'seq'))
- grad_wdown: float32 [2, 2048, 512], P(None, ('dp', 'seq'))
- grad_gains: float32 [2, 2, 512], P(None, None, ('dp', 'seq'))
- grad_biases: float32 [2, 6, 512], P(None, None, ('dp', 'seq'))
- grad_upbias: float32 [2, 2048], P(None, ('dp', 'seq'))
Inputs may be any that keep to these rules, and one draw needn't show every extreme that they name: `prefix_len`: the number of leading positions of a row whose incoming gradient is zero.
All inputs are finite; a program needn't handle non-finite values.
Results may differ from a plain program's by a relative error of at most 0.009.
Values may be sent and summed in bfloat16 or wider, within the bound.
A program may use at most 320 MiB of HBM per device.

v0:
```python
from functools import partial
from functools import reduce

import jax
import jax.numpy as jnp
from jax import lax
from jax.sharding import PartitionSpec as P

HDIM = 64
BLOCK = 16
LEVELS = 6
LAYERS = 2


def from_behind(array, axis, by):
    count = lax.axis_size(axis)
    pairs = [(i, i + by) for i in range(count) if 0 <= i + by < count]
    return lax.ppermute(array, axis, pairs)


def layer_norm(values, gain, shift):
    centred = values - jnp.mean(values, axis=-1, keepdims=True)
    spread = jnp.mean(centred * centred, axis=-1, keepdims=True)
    return centred * lax.rsqrt(spread + 1e-05) * gain + shift


def coarsen(field):
    return 0.5 * (field[:, 0::2] + field[:, 1::2])


def windows(field, rows):
    blocks = field.shape[1] // BLOCK - 2
    stacked = field.reshape(rows, blocks + 2, BLOCK, field.shape[2], field.shape[3])
    return jnp.concatenate([stacked[:, :-2], stacked[:, 1:-1], stacked[:, 2:]], axis=2)


def fold_windows(grads):
    rows, blocks = (grads.shape[0], grads.shape[1])
    rest = ((0, 0), (0, 0), (0, 0))
    total = jnp.pad(grads[:, :, :BLOCK], ((0, 0), (0, 2)) + rest)
    total = total + jnp.pad(grads[:, :, BLOCK : 2 * BLOCK], ((0, 0), (1, 1)) + rest)
    total = total + jnp.pad(grads[:, :, 2 * BLOCK :], ((0, 0), (2, 0)) + rest)
    return total.reshape(rows, (blocks + 2) * BLOCK, grads.shape[3], grads.shape[4])


def key_mask(blocks, offset, total, level_id):
    places = jnp.arange(3 * BLOCK, dtype=jnp.int32) // BLOCK
    owners = jnp.arange(blocks, dtype=jnp.int32)[:, None] + offset + places[None, :] - 1
    inside = (owners >= 0) & (owners < total)
    if level_id > 0:
        inside = inside & (places[None, :] != 1)
    return inside


def weigh(scores, inside, factor):
    masked = jnp.where(inside, scores, -1e30)
    peak_rows = jnp.max(masked, axis=-1)
    weights = jnp.where(inside, jnp.exp(masked - peak_rows[..., None]), 0.0)
    return (weights, peak_rows, factor * jnp.sum(weights, axis=-1))


def combine(numers, maxima, level_sums, axis):
    stretched = [
        jnp.repeat(piece_max, 2**level_id, axis=axis) for level_id, piece_max in enumerate(maxima)
    ]
    summit = reduce(jnp.maximum, stretched)
    numerator = jnp.zeros_like(numers[0])
    denominator = jnp.zeros_like(maxima[0])
    for level_id in range(len(numers)):
        scaling = jnp.exp(stretched[level_id] - summit)
        numerator = numerator + scaling[..., None] * jnp.repeat(
            numers[level_id], 2**level_id, axis=axis
        )
        denominator = denominator + scaling * jnp.repeat(
            level_sums[level_id], 2**level_id, axis=axis
        )
    return numerator / denominator[..., None]


def attend_forward(queries, key_rows, value_rows):
    rows, length, head_count, head_width = queries.shape
    model = head_count * head_width
    scaling = head_width ** (-0.5)
    top = LEVELS - 1
    query_levels, key_levels, value_levels = ([queries], [key_rows], [value_rows])
    for level_id in range(1, LEVELS):
        query_levels.append(coarsen(query_levels[-1].astype(jnp.float32)).astype(jnp.bfloat16))
        key_levels.append(coarsen(key_levels[-1].astype(jnp.float32)).astype(jnp.bfloat16))
        value_levels.append(coarsen(value_levels[-1].astype(jnp.float32)).astype(jnp.bfloat16))
    lower_rims = jnp.stack(
        [
            jnp.stack(
                [key_levels[level_id][:, -BLOCK:], value_levels[level_id][:, -BLOCK:]], axis=1
            )
            for level_id in range(top)
        ],
        axis=1,
    ).reshape(rows, top, 2, BLOCK, model)
    upper_rims = jnp.stack(
        [
            jnp.stack([key_levels[level_id][:, :BLOCK], value_levels[level_id][:, :BLOCK]], axis=1)
            for level_id in range(top)
        ],
        axis=1,
    ).reshape(rows, top, 2, BLOCK, model)
    from_lower = from_behind(lower_rims, "seq", 1).reshape(
        rows, top, 2, BLOCK, head_count, head_width
    )
    from_upper = from_behind(upper_rims, "seq", -1).reshape(
        rows, top, 2, BLOCK, head_count, head_width
    )
    whole_keys, whole_values = (
        lax.all_gather(key_levels[top], "seq", axis=1, tiled=True),
        lax.all_gather(value_levels[top], "seq", axis=1, tiled=True),
    )
    numers, maxima, level_sums, kept = ([], [], [], [])
    for level_id in range(top):
        factor = 2.0**level_id
        blocks = query_levels[level_id].shape[1] // BLOCK
        key_ext = jnp.concatenate(
            [from_lower[:, level_id, 0], key_levels[level_id], from_upper[:, level_id, 0]], axis=1
        )
        value_ext = jnp.concatenate(
            [from_lower[:, level_id, 1], value_levels[level_id], from_upper[:, level_id, 1]], axis=1
        )
        key_windows = windows(key_ext, rows)
        value_windows = windows(value_ext, rows)
        query_blocks = query_levels[level_id].reshape(rows, blocks, BLOCK, head_count, head_width)
        scores = (
            jnp.einsum(
                "rbihd,rbjhd->rbhij", query_blocks, key_windows, preferred_element_type=jnp.float32
            )
            * scaling
        )
        inside = key_mask(
            blocks, lax.axis_index("seq") * blocks, blocks * lax.axis_size("seq"), level_id
        )[None, :, None, None, :]
        weights, peak_rows, totals = weigh(scores, inside, factor)
        numer_blk = factor * jnp.einsum(
            "rbhij,rbjhd->rbihd",
            weights.astype(jnp.bfloat16),
            value_windows,
            preferred_element_type=jnp.float32,
        )
        numers.append(numer_blk.reshape(rows, blocks * BLOCK, head_count, head_width))
        maxima.append(peak_rows.transpose(0, 1, 3, 2).reshape(rows, blocks * BLOCK, head_count))
        level_sums.append(totals.transpose(0, 1, 3, 2).reshape(rows, blocks * BLOCK, head_count))
        kept.append((query_blocks, key_windows, value_windows, scores, inside))
    factor = 2.0**top
    count = query_levels[top].shape[1]
    total_keys = whole_keys.shape[1]
    query_place = (lax.axis_index("seq") * count + jnp.arange(count, dtype=jnp.int32)) // BLOCK
    key_place = jnp.arange(total_keys, dtype=jnp.int32) // BLOCK
    inside = (jnp.abs(query_place[:, None] - key_place[None, :]) == 1)[None, None]
    scores = (
        jnp.einsum(
            "rihd,rjhd->rhij", query_levels[top], whole_keys, preferred_element_type=jnp.float32
        )
        * scaling
    )
    weights, peak_rows, totals = weigh(scores, inside, factor)
    numer_top = factor * jnp.einsum(
        "rhij,rjhd->rihd",
        weights.astype(jnp.bfloat16),
        whole_values,
        preferred_element_type=jnp.float32,
    )
    numers.append(numer_top)
    maxima.append(peak_rows.transpose(0, 2, 1))
    level_sums.append(totals.transpose(0, 2, 1))
    kept.append((query_levels[top], whole_keys, whole_values, scores, inside))
    return (combine(numers, maxima, level_sums, 1), (numers, maxima, level_sums, kept))


def attend_backward(saved, grad_attended):
    numers, maxima, level_sums, kept = saved
    rows, length, head_count, head_width = grad_attended.shape
    model = head_count * head_width
    scaling = head_width ** (-0.5)
    top = LEVELS - 1
    _, mix_pull = jax.vjp(partial(combine, axis=1), numers, maxima, level_sums)
    grad_numers, grad_maxima, grad_sums = mix_pull(grad_attended)
    query_grads, lower_parts, upper_parts, key_mids, value_mids = ([], [], [], [], [])
    for level_id in range(top):
        query_blocks, key_windows, value_windows, scores, inside = kept[level_id]
        blocks = query_blocks.shape[1]
        factor = 2.0**level_id

        def level_weigh(score_blk, inside=inside, factor=factor):
            return weigh(score_blk, inside, factor)

        weigh_out, weigh_pull = jax.vjp(level_weigh, scores)
        grad_numer = (
            grad_numers[level_id]
            .astype(jnp.bfloat16)
            .reshape(rows, blocks, BLOCK, head_count, head_width)
        )
        grad_weights = factor * jnp.einsum(
            "rbihd,rbjhd->rbhij", grad_numer, value_windows, preferred_element_type=jnp.float32
        )
        grad_value_win = factor * jnp.einsum(
            "rbhij,rbihd->rbjhd",
            weigh_out[0].astype(jnp.bfloat16),
            grad_numer,
            preferred_element_type=jnp.float32,
        )
        grad_peak = (
            grad_maxima[level_id].reshape(rows, blocks, BLOCK, head_count).transpose(0, 1, 3, 2)
        )
        grad_total = (
            grad_sums[level_id].reshape(rows, blocks, BLOCK, head_count).transpose(0, 1, 3, 2)
        )
        grad_scores = weigh_pull((grad_weights, grad_peak, grad_total))[0].astype(jnp.bfloat16)
        grad_query = scaling * jnp.einsum(
            "rbhij,rbjhd->rbihd", grad_scores, key_windows, preferred_element_type=jnp.float32
        )
        query_grads.append(grad_query.reshape(rows, blocks * BLOCK, head_count, head_width))
        grad_key_ext = fold_windows(
            scaling
            * jnp.einsum(
                "rbhij,rbihd->rbjhd", grad_scores, query_blocks, preferred_element_type=jnp.float32
            )
        )
        grad_value_ext = fold_windows(grad_value_win)
        lower_parts.append(jnp.stack([grad_key_ext[:, :BLOCK], grad_value_ext[:, :BLOCK]], axis=1))
        upper_parts.append(
            jnp.stack([grad_key_ext[:, -BLOCK:], grad_value_ext[:, -BLOCK:]], axis=1)
        )
        key_mids.append(grad_key_ext[:, BLOCK:-BLOCK])
        value_mids.append(grad_value_ext[:, BLOCK:-BLOCK])
    query_top, whole_keys, whole_values, scores, inside = kept[top]
    factor = 2.0**top

    def top_weigh(score_blk):
        return weigh(score_blk, inside, factor)

    weigh_out, weigh_pull = jax.vjp(top_weigh, scores)
    grad_numer = grad_numers[top].astype(jnp.bfloat16)
    grad_weights = factor * jnp.einsum(
        "rihd,rjhd->rhij", grad_numer, whole_values, preferred_element_type=jnp.float32
    )
    grad_whole_values = factor * jnp.einsum(
        "rhij,rihd->rjhd",
        weigh_out[0].astype(jnp.bfloat16),
        grad_numer,
        preferred_element_type=jnp.float32,
    )
    grad_peak = grad_maxima[top].transpose(0, 2, 1)
    grad_total = grad_sums[top].transpose(0, 2, 1)
    grad_scores = weigh_pull((grad_weights, grad_peak, grad_total))[0].astype(jnp.bfloat16)
    query_carry = scaling * jnp.einsum(
        "rhij,rjhd->rihd", grad_scores, whole_keys, preferred_element_type=jnp.float32
    )
    grad_whole_keys = scaling * jnp.einsum(
        "rhij,rihd->rjhd", grad_scores, query_top, preferred_element_type=jnp.float32
    )
    key_carry, value_carry = (
        lax.psum_scatter(
            grad_whole_keys.astype(jnp.bfloat16), "seq", scatter_dimension=1, tiled=True
        ).astype(jnp.float32),
        lax.psum_scatter(
            grad_whole_values.astype(jnp.bfloat16), "seq", scatter_dimension=1, tiled=True
        ).astype(jnp.float32),
    )
    to_lower = jnp.stack(lower_parts, axis=1).reshape(rows, top, 2, BLOCK, model)
    to_upper = jnp.stack(upper_parts, axis=1).reshape(rows, top, 2, BLOCK, model)
    back_upper = (
        from_behind(to_lower.astype(jnp.bfloat16), "seq", -1)
        .astype(to_lower.dtype)
        .reshape(rows, top, 2, BLOCK, head_count, head_width)
    )
    back_lower = (
        from_behind(to_upper.astype(jnp.bfloat16), "seq", 1)
        .astype(to_upper.dtype)
        .reshape(rows, top, 2, BLOCK, head_count, head_width)
    )
    for level_id in reversed(range(top)):
        length_now = key_mids[level_id].shape[1]
        pad_start = ((0, 0), (0, length_now - BLOCK), (0, 0), (0, 0))
        pad_end = ((0, 0), (length_now - BLOCK, 0), (0, 0), (0, 0))
        key_now = (
            key_mids[level_id]
            + jnp.pad(back_lower[:, level_id, 0], pad_start)
            + jnp.pad(back_upper[:, level_id, 0], pad_end)
        )
        value_now = (
            value_mids[level_id]
            + jnp.pad(back_lower[:, level_id, 1], pad_start)
            + jnp.pad(back_upper[:, level_id, 1], pad_end)
        )
        query_now = query_grads[level_id] + 0.5 * jnp.repeat(query_carry, 2, axis=1)
        key_now = key_now + 0.5 * jnp.repeat(key_carry, 2, axis=1)
        value_now = value_now + 0.5 * jnp.repeat(value_carry, 2, axis=1)
        query_carry, key_carry, value_carry = (query_now, key_now, value_now)
    return (query_carry, key_carry, value_carry)


def layer_forward(inputs, weights_now, rows):
    w_qkv, w_out, w_up, w_down, norm_gains, bias_rows, up_bias = weights_now
    tokens, model = inputs.shape
    gains = norm_gains.astype(jnp.float32)
    biases = bias_rows.astype(jnp.float32)
    normed = layer_norm(inputs, gains[0], biases[0]).astype(jnp.bfloat16)
    mixed = jnp.dot(normed, w_qkv, preferred_element_type=jnp.float32)
    four_d = (rows, tokens // rows, model // HDIM, HDIM)
    queries = (mixed[:, :model] + biases[1]).astype(jnp.bfloat16).reshape(four_d)
    key_rows = mixed[:, model : 2 * model].astype(jnp.bfloat16).reshape(four_d)
    value_rows = (mixed[:, 2 * model :] + biases[2]).astype(jnp.bfloat16).reshape(four_d)
    attended, saved = attend_forward(queries, key_rows, value_rows)
    attended = attended.reshape(tokens, model).astype(jnp.bfloat16)
    middle = inputs + jnp.dot(attended, w_out, preferred_element_type=jnp.float32) + biases[3]
    second = layer_norm(middle, gains[1], biases[4]).astype(jnp.bfloat16)
    hidden = jnp.dot(second, w_up, preferred_element_type=jnp.float32) + up_bias.astype(jnp.float32)
    active = jax.nn.gelu(hidden, approximate=True).astype(jnp.bfloat16)
    output = middle + jnp.dot(active, w_down, preferred_element_type=jnp.float32) + biases[5]
    return (output, (normed, attended, saved, middle, second, hidden, active))


def layer_backward(inputs, weights_now, kept, grad_output, rows):
    w_qkv, w_out, w_up, w_down, norm_gains, bias_rows, up_bias = weights_now
    normed, attended, saved, middle, second, hidden, active = kept
    tokens, model = inputs.shape
    gains = norm_gains.astype(jnp.float32)
    biases = bias_rows.astype(jnp.float32)
    grad_branch = grad_output.astype(jnp.bfloat16)
    grad_down = jnp.einsum("nf,nd->fd", active, grad_branch, preferred_element_type=jnp.float32)
    grad_bias_five = jnp.sum(grad_branch.astype(jnp.float32), axis=0)
    grad_active = jnp.einsum("nd,fd->nf", grad_branch, w_down, preferred_element_type=jnp.float32)
    _, gelu_pull = jax.vjp(partial(jax.nn.gelu, approximate=True), hidden)
    grad_hidden = gelu_pull(grad_active)[0].astype(jnp.bfloat16)
    grad_up = jnp.einsum("nd,nf->df", second, grad_hidden, preferred_element_type=jnp.float32)
    grad_upbias = jnp.sum(grad_hidden.astype(jnp.float32), axis=0)
    grad_second = jnp.einsum("nf,df->nd", grad_hidden, w_up, preferred_element_type=jnp.float32)
    _, norm_pull = jax.vjp(layer_norm, middle, gains[1], biases[4])
    grad_mid_norm, grad_gain_two, grad_bias_four = norm_pull(grad_second)
    grad_middle = grad_output + grad_mid_norm
    grad_attn_branch = grad_middle.astype(jnp.bfloat16)
    grad_wout = jnp.einsum(
        "nd,ne->de", attended, grad_attn_branch, preferred_element_type=jnp.float32
    )
    grad_bias_three = jnp.sum(grad_attn_branch.astype(jnp.float32), axis=0)
    grad_attended = jnp.einsum(
        "ne,de->nd", grad_attn_branch, w_out, preferred_element_type=jnp.float32
    )
    grad_attended = lax.optimization_barrier(grad_attended.astype(jnp.bfloat16)).astype(jnp.float32)
    grad_attended = grad_attended.reshape(rows, tokens // rows, model // HDIM, HDIM)
    grad_query, grad_key, grad_value = attend_backward(saved, grad_attended)
    grad_mixed = jnp.concatenate(
        [
            grad_query.reshape(tokens, model),
            grad_key.reshape(tokens, model),
            grad_value.reshape(tokens, model),
        ],
        axis=1,
    ).astype(jnp.bfloat16)
    grad_bias_one = jnp.sum(grad_mixed[:, :model].astype(jnp.float32), axis=0)
    grad_bias_two = jnp.sum(grad_mixed[:, 2 * model :].astype(jnp.float32), axis=0)
    grad_wqkv = jnp.einsum("nd,ne->de", normed, grad_mixed, preferred_element_type=jnp.float32)
    grad_normed = jnp.einsum("ne,de->nd", grad_mixed, w_qkv, preferred_element_type=jnp.float32)
    _, first_pull = jax.vjp(layer_norm, inputs, gains[0], biases[0])
    grad_in_norm, grad_gain_one, grad_bias_zero = first_pull(grad_normed)
    grad_inputs = grad_middle + grad_in_norm
    grad_gains = jnp.stack([grad_gain_one, grad_gain_two], axis=0)
    grad_biases = jnp.stack(
        [
            grad_bias_zero,
            grad_bias_one,
            grad_bias_two,
            grad_bias_three,
            grad_bias_four,
            grad_bias_five,
        ],
        axis=0,
    )
    return (
        grad_inputs,
        (grad_wqkv, grad_wout, grad_up, grad_down, grad_gains, grad_biases, grad_upbias),
    )


def fetch_layer(shards, layer_id):
    w_qkv, w_out, w_up, w_down, norm_gains, bias_rows, up_bias = shards
    return (
        lax.all_gather(w_qkv[layer_id], ("dp", "seq"), axis=0, tiled=True),
        lax.all_gather(w_out[layer_id], ("dp", "seq"), axis=0, tiled=True),
        lax.all_gather(w_up[layer_id], ("dp", "seq"), axis=0, tiled=True),
        lax.all_gather(w_down[layer_id], ("dp", "seq"), axis=0, tiled=True),
        lax.all_gather(norm_gains[layer_id], ("dp", "seq"), axis=1, tiled=True),
        lax.all_gather(bias_rows[layer_id], ("dp", "seq"), axis=1, tiled=True),
        lax.all_gather(up_bias[layer_id], ("dp", "seq"), axis=0, tiled=True),
    )


def add_tuples(first, second):
    if first is None:
        return second
    return tuple((left + right for left, right in zip(first, second)))


def on_device(
    tokens_in, grad_output, prefix_len, w_qkv, w_out, w_up, w_down, norm_gains, bias_rows, up_bias
):
    micro, rows, local_len, model = tokens_in.shape
    shards = (w_qkv, w_out, w_up, w_down, norm_gains, bias_rows, up_bias)
    positions = lax.axis_index("seq") * local_len + jnp.arange(local_len, dtype=jnp.int32)
    layer_sums = [None] * LAYERS
    outputs, grad_inputs = ([], [])
    for micro_id in range(micro):
        state = tokens_in[micro_id].astype(jnp.float32).reshape(rows * local_len, model)
        layer_inputs, layer_kept = ([], [])
        for layer_id in range(LAYERS):
            layer_inputs.append(state)
            state, kept_now = layer_forward(state, fetch_layer(shards, layer_id), rows)
            layer_kept.append(kept_now)
        outputs.append(state.astype(jnp.bfloat16).reshape(rows, local_len, model))
        keep_rows = (positions[None, :] >= prefix_len[micro_id][:, None]).astype(jnp.float32)
        grad_state = (grad_output[micro_id].astype(jnp.float32) * keep_rows[..., None]).reshape(
            rows * local_len, model
        )
        for layer_id in reversed(range(LAYERS)):
            weights_now = fetch_layer(shards, layer_id)
            grad_state, layer_grads = layer_backward(
                layer_inputs[layer_id], weights_now, layer_kept[layer_id], grad_state, rows
            )
            grad_qkv, grad_wout, grad_wup, grad_wdown, grad_gains, grad_biases, grad_upbias = (
                layer_grads
            )
            owned = (
                lax.psum_scatter(grad_qkv, ("dp", "seq"), scatter_dimension=0, tiled=True),
                lax.psum_scatter(grad_wout, ("dp", "seq"), scatter_dimension=0, tiled=True),
                lax.psum_scatter(grad_wup, ("dp", "seq"), scatter_dimension=0, tiled=True),
                lax.psum_scatter(grad_wdown, ("dp", "seq"), scatter_dimension=0, tiled=True),
                lax.psum_scatter(grad_gains, ("dp", "seq"), scatter_dimension=1, tiled=True),
                lax.psum_scatter(grad_biases, ("dp", "seq"), scatter_dimension=1, tiled=True),
                lax.psum_scatter(grad_upbias, ("dp", "seq"), scatter_dimension=0, tiled=True),
            )
            layer_sums[layer_id] = add_tuples(layer_sums[layer_id], owned)
        grad_inputs.append(grad_state.reshape(rows, local_len, model))
    stacked = tuple(
        (
            jnp.stack([layer_sums[layer_id][index_id] for layer_id in range(LAYERS)], axis=0)
            for index_id in range(7)
        )
    )
    return (
        jnp.stack(outputs, axis=0),
        jnp.stack(grad_inputs, axis=0),
        stacked[0],
        stacked[1],
        stacked[2],
        stacked[3],
        stacked[4],
        stacked[5],
        stacked[6],
    )


def solution(mesh):
    in_specs = (
        P(None, "dp", "seq", None),
        P(None, "dp", "seq", None),
        P(None, "dp"),
        P(None, ("dp", "seq"), None),
        P(None, ("dp", "seq"), None),
        P(None, ("dp", "seq"), None),
        P(None, ("dp", "seq"), None),
        P(None, None, ("dp", "seq")),
        P(None, None, ("dp", "seq")),
        P(None, ("dp", "seq")),
    )
    out_specs = (
        P(None, "dp", "seq", None),
        P(None, "dp", "seq", None),
        P(None, ("dp", "seq"), None),
        P(None, ("dp", "seq"), None),
        P(None, ("dp", "seq"), None),
        P(None, ("dp", "seq"), None),
        P(None, None, ("dp", "seq")),
        P(None, None, ("dp", "seq")),
        P(None, ("dp", "seq")),
    )
    return jax.shard_map(
        on_device, mesh=mesh, in_specs=in_specs, out_specs=out_specs, check_vma=False
    )
```

profile of v0, /device:TPU:0, one launch (start us, length us, event | category | flops | bytes accessed | tf_op | source)
XLA Modules:
  0.0 3854.2 jit_solution(11578816982808127693)
XLA Ops:
  25.3 42.5 %all-reduce.189 = (bf16[2048]{0:T(1024)(128)(2,1)S(1)}, bf16[2048]{0:T(1024)(128)(2,1)S(1)}) all-reduce(bf16[2048]{0:T(1024)(128)(2,1)S(1)} %dynamic-update-slice, bf16[2048]{0:T(1024)(128)(2,1)S(1)} %dynamic-update-slice.1), channel_id=7, replica_groups=mesh['dp'=8,'seq'=4] {'dp','seq'}, use_global_device_ids=true, to_apply=%add.184 | all-reduce | flops 4096 | bytes 16384
  69.4 41.0 %all-gather = bf16[1,2,512]{1,0,2:T(2,128)(2,1)S(1)} all-gather(bf16[1,2,16]{1,0,2:T(2,128)(2,1)S(1)} %copy.12413), channel_id=2, replica_groups=mesh['dp'=8,'seq'=4] {'dp','seq'}, dimensions={2}, use_global_device_ids=true | all-gather | bytes 2112 | tf_op jit(solution)/shard_map/all_gather | solution.py:388
  114.0 37.7 all-gather.1
  152.0 11.8 slice_reduce_fusion.9
  163.9 38.8 %all-gather.7 = bf16[1,2,512]{1,0,2:T(2,128)(2,1)S(1)} all-gather(bf16[1,2,16]{1,0,2:T(2,128)(2,1)S(1)} %copy.12467), channel_id=9, replica_groups=mesh['dp'=8,'seq'=4] {'dp','seq'}, dimensions={2}, use_global_device_ids=true | all-gather | bytes 2112 | tf_op jit(solution)/shard_map/all_gather | solution.py:388
  206.3 37.8 all-gather.8
  244.4 11.8 slice_reduce_fusion.1
  256.2 42.6 %all-gather.10 = bf16[1,512,512]{2,1,0:T(8,128)(2,1)} all-gather(bf16[1,16,512]{2,1,0:T(8,128)(2,1)S(1)} %get-tuple-element.1017), channel_id=12, replica_groups=mesh['dp'=8,'seq'=4] {'dp','seq'}, dimensions={1}, use_global_device_ids=true | all-gather | bytes 540672 | tf_op jit(solution)/shard_map/all_gather | solution.py:385
  298.8 38.2 all-gather.3
  340.6 4.9 slice.2649
  359.3 5.1 slice.2652
  418.5 9.7 slice.2684
  428.3 9.7 slice.2685
  446.8 10.1 slice.2462
  456.9 10.3 slice.2463
  480.1 5.3 all_gather.118
  498.1 5.3 all_gather.119
  513.3 5.3 all_gather.48
  527.3 5.3 all_gather.47
  835.9 4.7 slice.2542
  869.2 4.9 slice.2544
  911.0 9.8 slice.2783
  920.8 10.3 slice.2784
  937.7 8.8 slice.2576
  946.5 9.6 slice.2577
  967.6 6.6 all_gather.112
  985.7 5.6 all_gather.121
  1001.8 5.3 all_gather.113
  1015.2 5.3 all_gather.120
  1309.1 4.9 convert_reduce_fusion.1
  1579.5 7.1 reduce-scatter.61.cloned.1.call-done
  1778.1 4.8 convert_reduce_fusion.3
  1786.9 8.9 reduce-scatter.69.cloned.1.call-done
  2032.1 5.3 convolution_bitcast_fusion.2
  2240.1 15.6 reduce-scatter.67.cloned.1.call-done
  2257.0 20.9 reduce-scatter.65.cloned.1.call-done
  2387.4 39.5 %all-reduce.188 = (f32[2048]{0:T(1024)S(1)}, f32[2048]{0:T(1024)S(1)}) all-reduce(f32[2048]{0:T(1024)S(1)} %add.3637, f32[2048]{0:T(1024)S(1)} %add.3636), channel_id=51, replica_groups=mesh['dp'=8,'seq'=4] {'dp','seq'}, use_global_device_ids=true, to_apply=%region_293.294.clone | all-reduce | flops 4096 | bytes 32768
  2428.5 117.4 %reduce-scatter.83.cloned.1.call-done = f32[16,6]{1,0:T(8,128)} async-done(((f32[512,6]{1,0:T(8,128)}), f32[16,6]{1,0:T(8,128)}) %reduce-scatter.83.cloned.1.call-update) | async-done | bytes 400
  2549.4 128.3 %reduce-scatter.77.cloned.1.call-done = f32[16,2]{1,0:T(8,128)} async-done(((f32[512,2]{1,0:T(8,128)}), f32[16,2]{1,0:T(8,128)}) %reduce-scatter.77.cloned.1.call-update) | async-done | bytes 144
  2679.1 131.1 %reduce-scatter.81.cloned.1.call-done = f32[16,6]{1,0:T(8,128)} async-done(((f32[512,6]{1,0:T(8,128)}), f32[16,6]{1,0:T(8,128)}) %reduce-scatter.81.cloned.1.call-update) | async-done | bytes 400
  2811.6 132.0 %reduce-scatter.51.cloned.1.call-done = f32[16,512]{1,0:T(8,128)} async-done(((f32[512,512]{1,0:T(8,128)}), f32[16,512]{1,0:T(8,128)}) %reduce-scatter.51.cloned.1.call-update) | async-done | bytes 32784 | tf_op jit(solution)/shard_map/reduce_scatter | solution.py:430
  2943.6 133.3 %reduce-scatter.49.cloned.1.call-done = f32[16,512]{1,0:T(8,128)} async-done(((f32[512,512]{1,0:T(8,128)}), f32[16,512]{1,0:T(8,128)}) %reduce-scatter.49.cloned.1.call-update) | async-done | bytes 32784 | tf_op jit(solution)/shard_map/reduce_scatter | solution.py:430
  3078.3 101.5 %reduce-scatter.47.cloned.1.call-done = f32[16,1536]{1,0:T(8,128)} async-done(((f32[512,1536]{1,0:T(8,128)}), f32[16,1536]{1,0:T(8,128)}) %reduce-scatter.47.cloned.1.call-update) | async-done | bytes 98320 | tf_op jit(solution)/shard_map/reduce_scatter | solution.py:429
  3179.8 105.9 %reduce-scatter.45.cloned.1.call-done = f32[16,1536]{1,0:T(8,128)} async-done(((f32[512,1536]{1,0:T(8,128)}), f32[16,1536]{1,0:T(8,128)}) %reduce-scatter.45.cloned.1.call-update) | async-done | bytes 98320 | tf_op jit(solution)/shard_map/reduce_scatter | solution.py:429
  3287.3 141.2 %reduce-scatter.59.cloned.1.call-done = f32[64,512]{1,0:T(8,128)} async-done(((f32[2048,512]{1,0:T(8,128)}), f32[64,512]{1,0:T(8,128)}) %reduce-scatter.59.cloned.1.call-update) | async-done | bytes 131088 | tf_op jit(solution)/shard_map/reduce_scatter | solution.py:432
  3428.5 139.0 %reduce-scatter.57.cloned.1.call-done = f32[64,512]{1,0:T(8,128)} async-done(((f32[2048,512]{1,0:T(8,128)}), f32[64,512]{1,0:T(8,128)}) %reduce-scatter.57.cloned.1.call-update) | async-done | bytes 131088 | tf_op jit(solution)/shard_map/reduce_scatter | solution.py:432
  3569.1 137.7 %reduce-scatter.55.cloned.1.call-done = f32[16,2048]{1,0:T(8,128)} async-done(((f32[512,2048]{1,0:T(8,128)}), f32[16,2048]{1,0:T(8,128)}) %reduce-scatter.55.cloned.1.call-update) | async-done | bytes 131088 | tf_op jit(solution)/shard_map/reduce_scatter | solution.py:431
  3706.8 138.9 %reduce-scatter.53.cloned.1.call-done = f32[16,2048]{1,0:T(8,128)} async-done(((f32[512,2048]{1,0:T(8,128)}), f32[16,2048]{1,0:T(8,128)}) %reduce-scatter.53.cloned.1.call-update) | async-done | bytes 131088 | tf_op jit(solution)/shard_map/reduce_scatter | solution.py:431
  (5240 shorter events, 1861.9 us)
Async XLA Ops:
  7.2 329.9 %all-gather.21.cloned.1.call-start = ((), (), s32[]{:S(2)}) async-start(), calls=%async_computation.20 | async-start | bytes 1622016 | tf_op jit(solution)/shard_map/all_gather | solution.py:384
  8.7 811.4 %all-gather.23.cloned.1.call-start = ((), (), s32[]{:S(2)}) async-start(), calls=%async_computation.21 | async-start | bytes 2162688 | tf_op jit(solution)/shard_map/all_gather | solution.py:386
  10.3 813.6 %all-gather.25.cloned.1.call-start = ((), (), s32[]{:S(2)}) async-start(), calls=%async_computation.22 | async-start | bytes 2162688 | tf_op jit(solution)/shard_map/all_gather | solution.py:387
  11.9 815.5 %all-gather.27.cloned.1.call-start = ((), (), s32[]{:S(2)}) async-start(), calls=%async_computation.23 | async-start | bytes 1622016 | tf_op jit(solution)/shard_map/all_gather | solution.py:384
  12.5 1290.5 %all-gather.29.cloned.1.call-start = ((), (), s32[]{:S(2)}) async-start(), calls=%async_computation.24 | async-start | bytes 2162688 | tf_op jit(solution)/shard_map/all_gather | solution.py:386
  13.1 1296.0 %all-gather.31.cloned.1.call-start = ((), (), s32[]{:S(2)}) async-start(), calls=%async_computation.25 | async-start | bytes 2162688 | tf_op jit(solution)/shard_map/all_gather | solution.py:387
  13.7 1564.4 %reduce-scatter.63.cloned.1.call-start = ((), (), s32[]{:S(2)}) async-start(), calls=%async_computation.35 | async-start | bytes 40960
  23.4 313.7 %copy-start.1257 = (f32[256]{0:T(256)}, f32[256]{0:T(256)S(1)}, u32[]{:S(2)}) copy-start(f32[256]{0:T(256)S(1)} %get-tuple-element.1178) | copy-start | bytes 3076
  23.4 332.5 %copy-start.1248 = (f32[256]{0:T(256)}, f32[256]{0:T(256)S(1)}, u32[]{:S(2)}) copy-start(f32[256]{0:T(256)S(1)} %get-tuple-element.1179) | copy-start | bytes 3076
  24.7 331.1 %copy-start.1250 = (f32[256]{0:T(256)}, f32[256]{0:T(256)S(1)}, u32[]{:S(2)}) copy-start(f32[256]{0:T(256)S(1)} %fusion.953) | copy-start | bytes 3076
  24.8 312.3 %copy-start.1302 = (f32[256]{0:T(256)}, f32[256]{0:T(256)S(1)}, u32[]{:S(2)}) copy-start(f32[256]{0:T(256)S(1)} %fusion.957) | copy-start | bytes 3076
  337.0 474.4 %copy-start.10 = (bf16[1,512,512]{2,1,0:T(8,128)(2,1)}, bf16[1,512,512]{2,1,0:T(8,128)(2,1)S(1)}, u32[]{:S(2)}) copy-start(bf16[1,512,512]{2,1,0:T(8,128)(2,1)S(1)} %all-gather.3) | copy-start | bytes 1572868
  549.9 39.7 %collective-permute-start.4 = (bf16[1,5,2,16,512]{4,3,2,1,0:T(8,128)(2,1)}, bf16[1,5,2,16,512]{4,3,2,1,0:T(8,128)(2,1)}, u32[]{:S(2)}, u32[]{:S(2)}) collective-permute-start(bf16[1,5,2,16,512]{4,3,2,1,0:T(8,128)(2,1)} %constant_dynamic-update-slice_fusion.22), channel_id=1, source_target_pairs={{0,1},{1,2},{2,3},{4,5},{5,6},{6,7},{8,9},{9,10},{10,11},{12,13},{... | collective-permute-start | bytes 491528 | tf_op jit(solution)/shard_map/ppermute | solution.py:18
  552.8 38.7 %collective-permute-start.5 = (bf16[1,5,2,16,512]{4,3,2,1,0:T(8,128)(2,1)}, bf16[1,5,2,16,512]{4,3,2,1,0:T(8,128)(2,1)}, u32[]{:S(2)}, u32[]{:S(2)}) collective-permute-start(bf16[1,5,2,16,512]{4,3,2,1,0:T(8,128)(2,1)} %constant_dynamic-update-slice_fusion.27), channel_id=1, source_target_pairs={{1,0},{2,1},{3,2},{5,4},{6,5},{7,6},{9,8},{10,9},{11,10},{13,12},{... | collective-permute-start | bytes 491528 | tf_op jit(solution)/shard_map/ppermute | solution.py:18
  563.2 32.8 collective-permute-start
  567.1 30.7 collective-permute-start.1
  827.2 791.2 %copy-start.6 = (f32[256,512]{1,0:T(8,128)}, f32[256,512]{1,0:T(8,128)S(1)}, u32[]{:S(2)}) copy-start(f32[256,512]{1,0:T(8,128)S(1)} %get-tuple-element.1088) | copy-start | bytes 1572868
  1036.7 36.2 collective-permute-start.2
  1039.6 38.5 collective-permute-start.3
  1048.0 45.5 %collective-permute-start.6 = (bf16[1,5,2,16,512]{4,3,2,1,0:T(8,128)(2,1)}, bf16[1,5,2,16,512]{4,3,2,1,0:T(8,128)(2,1)}, u32[]{:S(2)}, u32[]{:S(2)}) collective-permute-start(bf16[1,5,2,16,512]{4,3,2,1,0:T(8,128)(2,1)} %constant_dynamic-update-slice_fusion.33), channel_id=1, source_target_pairs={{0,1},{1,2},{2,3},{4,5},{5,6},{6,7},{8,9},{9,10},{10,11},{12,13},{... | collective-permute-start | bytes 491528 | tf_op jit(solution)/shard_map/ppermute | solution.py:18
  1052.1 50.5 %collective-permute-start.7 = (bf16[1,5,2,16,512]{4,3,2,1,0:T(8,128)(2,1)}, bf16[1,5,2,16,512]{4,3,2,1,0:T(8,128)(2,1)}, u32[]{:S(2)}, u32[]{:S(2)}) collective-permute-start(bf16[1,5,2,16,512]{4,3,2,1,0:T(8,128)(2,1)} %constant_dynamic-update-slice_fusion.38), channel_id=1, source_target_pairs={{1,0},{2,1},{3,2},{5,4},{6,5},{7,6},{9,8},{10,9},{11,10},{13,12},{... | collective-permute-start | bytes 491528 | tf_op jit(solution)/shard_map/ppermute | solution.py:18
  1508.3 78.4 %reduce-scatter.61.cloned.1.call-start = ((), (), s32[]{:S(2)}) async-start(), calls=%async_computation.34 | async-start | bytes 40960
  1555.7 40.0 %collective-permute-start.8 = (bf16[1,5,2,16,512]{4,3,2,1,0:T(8,128)(2,1)}, bf16[1,5,2,16,512]{4,3,2,1,0:T(8,128)(2,1)}, u32[]{:S(2)}, u32[]{:S(2)}) collective-permute-start(bf16[1,5,2,16,512]{4,3,2,1,0:T(8,128)(2,1)} %constant_dynamic-update-slice_fusion.44), channel_id=1, source_target_pairs={{0,1},{1,2},{2,3},{4,5},{5,6},{6,7},{8,9},{9,10},{10,11},{12,13},{... | collective-permute-start | bytes 491528 | tf_op jit(solution)/shard_map/ppermute | solution.py:18
  1566.7 21.3 collective-permute-start.9
  1568.0 217.4 %reduce-scatter.71.cloned.1.call-start = ((), (), s32[]{:S(2)}) async-start(), calls=%async_computation.39 | async-start | bytes 40960
  1723.2 72.6 %reduce-scatter.69.cloned.1.call-start = ((), (), s32[]{:S(2)}) async-start(), calls=%async_computation.38 | async-start | bytes 40960
  1762.9 41.8 %collective-permute-start.12 = (bf16[1,5,2,16,512]{4,3,2,1,0:T(8,128)(2,1)}, bf16[1,5,2,16,512]{4,3,2,1,0:T(8,128)(2,1)}, u32[]{:S(2)}, u32[]{:S(2)}) collective-permute-start(bf16[1,5,2,16,512]{4,3,2,1,0:T(8,128)(2,1)} %constant_dynamic-update-slice_fusion.64), channel_id=1, source_target_pairs={{0,1},{1,2},{2,3},{4,5},{5,6},{6,7},{8,9},{9,10},{10,11},{12,13},{... | collective-permute-start | bytes 491528 | tf_op jit(solution)/shard_map/ppermute | solution.py:18
  1771.6 25.6 collective-permute-start.13
  1774.0 463.3 %reduce-scatter.75.cloned.1.call-start = ((), (), s32[]{:S(2)}) async-start(), calls=%async_computation.41 | async-start | bytes 40960
  2068.1 170.5 %reduce-scatter.73.cloned.1.call-start = ((), (), s32[]{:S(2)}) async-start(), calls=%async_computation.40 | async-start | bytes 40960
  2198.6 87.1 %collective-permute-start.10 = (bf16[1,5,2,16,512]{4,3,2,1,0:T(8,128)(2,1)}, bf16[1,5,2,16,512]{4,3,2,1,0:T(8,128)(2,1)}, u32[]{:S(2)}, u32[]{:S(2)}) collective-permute-start(bf16[1,5,2,16,512]{4,3,2,1,0:T(8,128)(2,1)} %constant_dynamic-update-slice_fusion.54), channel_id=1, source_target_pairs={{0,1},{1,2},{2,3},{4,5},{5,6},{6,7},{8,9},{9,10},{10,11},{12,13},{... | collective-permute-start | bytes 491528 | tf_op jit(solution)/shard_map/ppermute | solution.py:18
  2205.8 73.6 %collective-permute-start.11 = (bf16[1,5,2,16,512]{4,3,2,1,0:T(8,128)(2,1)}, bf16[1,5,2,16,512]{4,3,2,1,0:T(8,128)(2,1)}, u32[]{:S(2)}, u32[]{:S(2)}) collective-permute-start(bf16[1,5,2,16,512]{4,3,2,1,0:T(8,128)(2,1)} %constant_dynamic-update-slice_fusion.59), channel_id=1, source_target_pairs={{1,0},{2,1},{3,2},{5,4},{6,5},{7,6},{9,8},{10,9},{11,10},{13,12},{... | collective-permute-start | bytes 491528 | tf_op jit(solution)/shard_map/ppermute | solution.py:18
  2212.0 43.7 %reduce-scatter.67.cloned.1.call-start = ((), (), s32[]{:S(2)}) async-start(), calls=%async_computation.37 | async-start | bytes 40960
  2216.6 61.4 %reduce-scatter.65.cloned.1.call-start = ((), (), s32[]{:S(2)}) async-start(), calls=%async_computation.36 | async-start | bytes 40960
  2218.3 209.4 %reduce-scatter.79.cloned.1.call-start = ((), (), s32[]{:S(2)}) async-start(), calls=%async_computation.43 | async-start | bytes 270336
  2223.6 91.8 %collective-permute-start.14 = (bf16[1,5,2,16,512]{4,3,2,1,0:T(8,128)(2,1)}, bf16[1,5,2,16,512]{4,3,2,1,0:T(8,128)(2,1)}, u32[]{:S(2)}, u32[]{:S(2)}) collective-permute-start(bf16[1,5,2,16,512]{4,3,2,1,0:T(8,128)(2,1)} %constant_dynamic-update-slice_fusion.74), channel_id=1, source_target_pairs={{0,1},{1,2},{2,3},{4,5},{5,6},{6,7},{8,9},{9,10},{10,11},{12,13},{... | collective-permute-start | bytes 491528 | tf_op jit(solution)/shard_map/ppermute | solution.py:18
  2227.3 318.6 %reduce-scatter.83.cloned.1.call-start = ((), (), s32[]{:S(2)}) async-start(), calls=%async_computation.45 | async-start | bytes 270336
  2231.9 65.8 %collective-permute-start.15 = (bf16[1,5,2,16,512]{4,3,2,1,0:T(8,128)(2,1)}, bf16[1,5,2,16,512]{4,3,2,1,0:T(8,128)(2,1)}, u32[]{:S(2)}, u32[]{:S(2)}) collective-permute-start(bf16[1,5,2,16,512]{4,3,2,1,0:T(8,128)(2,1)} %constant_dynamic-update-slice_fusion.79), channel_id=1, source_target_pairs={{1,0},{2,1},{3,2},{5,4},{6,5},{7,6},{9,8},{10,9},{11,10},{13,12},{... | collective-permute-start | bytes 491528 | tf_op jit(solution)/shard_map/ppermute | solution.py:18
  2233.2 444.5 %reduce-scatter.77.cloned.1.call-start = ((), (), s32[]{:S(2)}) async-start(), calls=%async_computation.42 | async-start | bytes 270336
  2339.3 471.0 %reduce-scatter.81.cloned.1.call-start = ((), (), s32[]{:S(2)}) async-start(), calls=%async_computation.44 | async-start | bytes 270336
  2340.5 603.1 %reduce-scatter.51.cloned.1.call-start = ((), (), s32[]{:S(2)}) async-start(), calls=%async_computation.29 | async-start | bytes 1081344 | tf_op jit(solution)/shard_map/reduce_scatter | solution.py:430
  2343.3 733.6 %reduce-scatter.49.cloned.1.call-start = ((), (), s32[]{:S(2)}) async-start(), calls=%async_computation.28 | async-start | bytes 1081344 | tf_op jit(solution)/shard_map/reduce_scatter | solution.py:430
  2346.9 832.8 %reduce-scatter.47.cloned.1.call-start = ((), (), s32[]{:S(2)}) async-start(), calls=%async_computation.27 | async-start | bytes 3244032 | tf_op jit(solution)/shard_map/reduce_scatter | solution.py:429
  2351.6 934.0 %reduce-scatter.45.cloned.1.call-start = ((), (), s32[]{:S(2)}) async-start(), calls=%async_computation.26 | async-start | bytes 3244032 | tf_op jit(solution)/shard_map/reduce_scatter | solution.py:429
  2356.2 1072.2 %reduce-scatter.59.cloned.1.call-start = ((), (), s32[]{:S(2)}) async-start(), calls=%async_computation.33 | async-start | bytes 4325376 | tf_op jit(solution)/shard_map/reduce_scatter | solution.py:432
  2363.3 1204.2 %reduce-scatter.57.cloned.1.call-start = ((), (), s32[]{:S(2)}) async-start(), calls=%async_computation.32 | async-start | bytes 4325376 | tf_op jit(solution)/shard_map/reduce_scatter | solution.py:432
  2369.5 1337.4 %reduce-scatter.55.cloned.1.call-start = ((), (), s32[]{:S(2)}) async-start(), calls=%async_computation.31 | async-start | bytes 4325376 | tf_op jit(solution)/shard_map/reduce_scatter | solution.py:431
  2375.7 1470.1 %reduce-scatter.53.cloned.1.call-start = ((), (), s32[]{:S(2)}) async-start(), calls=%async_computation.30 | async-start | bytes 4325376 | tf_op jit(solution)/shard_map/reduce_scatter | solution.py:431
  (1375 other events, 12768.5 us)
Sparse Core Ops, SparseCore 0:
  11.5 57.8 all-gather.20
  72.2 55.5 all-gather.22
  130.6 55.6 all-gather.24
  189.1 54.2 all-gather.26
  246.1 55.5 all-gather.28
  304.4 55.4 all-gather.30
  1508.4 18.5 reduce-scatter.62
  1568.1 18.4 reduce-scatter.60
  1723.3 19.3 reduce-scatter.70
  1774.1 21.6 reduce-scatter.68
  2068.3 19.3 reduce-scatter.74
  2212.1 21.6 reduce-scatter.72
  2236.2 19.3 reduce-scatter.66
  2258.6 19.3 reduce-scatter.64
  2280.1 133.8 reduce-scatter.78
  2416.1 129.7 reduce-scatter.82
  2548.0 129.7 reduce-scatter.76
  2680.5 129.7 reduce-scatter.80
  2812.5 131.0 reduce-scatter.50
  2945.8 131.0 reduce-scatter.48
  3082.3 97.4 reduce-scatter.46
  3185.2 100.4 reduce-scatter.44
  3288.0 140.4 reduce-scatter.58
  3430.6 136.8 reduce-scatter.56
  3569.7 137.0 reduce-scatter.54
  3709.0 136.7 reduce-scatter.52
where the time goes:
time: 3890 us; the launch traced here: 3850 us
  waiting for transfers between devices  1460 us (38%)
  local copies, waits for them, and re-layouts  1180 us (30%)
  other arithmetic  423 us (11%)
  blocking collectives  362 us (9%)
  matrix products  355 us (9%)
    unnamed x38, waiting for transfers between devices  431 us
    reduce_scatter x2, waiting for transfers between devices, on_device(): lax.psum_scatter(grad_wdown, ('dp', 'seq'), scatter_dimension=0, tiled=True)  280 us
    reduce_scatter x2, waiting for transfers between devices, on_device(): lax.psum_scatter(grad_wup, ('dp', 'seq'), scatter_dimension=0, tiled=True)  277 us
    reduce_scatter x2, waiting for transfers between devices, on_device(): lax.psum_scatter(grad_wout, ('dp', 'seq'), scatter_dimension=0, tiled=True)  265 us
    reduce_scatter x2, waiting for transfers between devices, on_device(): lax.psum_scatter(grad_qkv, ('dp', 'seq'), scatter_dimension=0, tiled=True)  207 us
    slice x120, local copies, waits for them, and re-layouts, coarsen(): return 0.5 * (field[:, 0::2] + field[:, 1::2])  178 us
    unnamed x3007, local copies, waits for them, and re-layouts  175 us
    broadcast_in_dim x80, local copies, waits for them, and re-layouts, combine(): jnp.repeat(numers[level_id], 2 ** level_id, axis=axis)  95.3 us

commit v1 on v0

v1 whole, which is shorter than its diff:
```python
import functools
import math

import jax
import jax.numpy as jnp
from jax import lax
from jax.experimental import pallas as pl
from jax.experimental.pallas import tpu as pltpu
from jax.sharding import PartitionSpec as P

HDIM = 64
BLOCK = 16
LEVELS = 6
LAYERS = 2
TOP = LEVELS - 1
CHUNK = 64
LN2 = math.log(2.0)
F32 = jnp.float32
BF16 = jnp.bfloat16
NEG = -1e30
VMEM_LIMIT = 60 * 2**20
AXES = ("dp", "seq")


def dot_nn(a, b):
    return lax.dot_general(a, b, (((1,), (0,)), ((), ())), preferred_element_type=F32)


def dot_nt(a, b):
    return lax.dot_general(a, b, (((1,), (1,)), ((), ())), preferred_element_type=F32)


def dot_tn(a, b):
    return lax.dot_general(a, b, (((0,), (0,)), ((), ())), preferred_element_type=F32)


class Sizes:
    def __init__(self, rows, run, model, hidden, seq):
        self.rows, self.run, self.model, self.hidden, self.seq = rows, run, model, hidden, seq
        self.tokens = rows * run
        self.pairs = model // 128
        self.chunks = run // CHUNK
        self.count = [run >> level for level in range(LEVELS)]
        self.top_keys = self.count[TOP] * seq
        self.offset, at = [], 0
        for level in range(TOP):
            self.offset.append(at)
            at += self.count[level] + 2 * BLOCK
        self.offset.append(at)
        self.bank = at + self.top_keys
        self.keys = [CHUNK + 2 * BLOCK, CHUNK // 2 + 2 * BLOCK] + [2 * BLOCK] * (TOP - 2) + [self.top_keys]
        self.start = [sum(self.keys[:level]) for level in range(LEVELS)]
        self.width = sum(self.keys)
        self.rim = rows * TOP * 2 * BLOCK


def normalise(values):
    centred = values - jnp.mean(values, axis=-1, keepdims=True)
    spread = jnp.mean(centred * centred, axis=-1, keepdims=True)
    inverse = lax.rsqrt(spread + 1e-05)
    return centred * inverse, inverse


def norm_back(grad, hat, inverse, gain):
    scaled = grad * gain
    first = jnp.mean(scaled, axis=-1, keepdims=True)
    second = jnp.mean(scaled * hat, axis=-1, keepdims=True)
    return inverse * (scaled - first - hat * second)


GELU_C = math.sqrt(2.0 / math.pi)


def gelu(v):
    return 0.5 * v * (1.0 + jnp.tanh(GELU_C * (v + 0.044715 * (v * v * v))))


def gelu_both(v):
    square = v * v
    t = jnp.tanh(GELU_C * (v + 0.044715 * (square * v)))
    half = 0.5 * (1.0 + t)
    slope = half + 0.5 * v * (1.0 - t * t) * (GELU_C * (1.0 + 3.0 * 0.044715 * square))
    return v * half, slope


def row_loop(total, step, body):
    def go(j, carry):
        body(pl.ds(pl.multiple_of(j * step, step), step))
        return carry

    lax.fori_loop(0, total // step, go, 0)


def coarse_matrix(run):
    row = lax.broadcasted_iota(jnp.int32, (run, run), 0)
    col = lax.broadcasted_iota(jnp.int32, (run, run), 1)
    out = jnp.zeros((run, run), F32)
    base = 0
    for level in range(1, LEVELS):
        n = run >> level
        hit = (row >= base) & (row < base + n) & ((col >> level) == row - base)
        out = jnp.where(hit, 2.0**-level, out)
        base += n
    return out.astype(BF16)


def spread_matrix():
    row = lax.broadcasted_iota(jnp.int32, (TOP * CHUNK, CHUNK), 0)
    col = lax.broadcasted_iota(jnp.int32, (TOP * CHUNK, CHUNK), 1)
    out = jnp.zeros((TOP * CHUNK, CHUNK), F32)
    for level in range(1, LEVELS):
        base = (level - 1) * CHUNK
        hit = (row >= base) & (row < base + CHUNK) & (((row - base) >> level) == (col >> level))
        out = jnp.where(hit, 2.0**-level, out)
    return out.astype(BF16)


def fill_mask(sz, mask_ref):
    place = lax.axis_index("seq")
    for i in range(sz.chunks):
        for level in range(LEVELS):
            shape = (sz.keys[level], 128)
            key = lax.broadcasted_iota(jnp.int32, shape, 0)
            token = lax.broadcasted_iota(jnp.int32, shape, 1) % CHUNK
            per_run = sz.count[level] // BLOCK
            if level == TOP:
                query_block = ((place * sz.run + i * CHUNK + token) >> TOP) // BLOCK
                allowed = jnp.abs(query_block - key // BLOCK) == 1
            else:
                own = (i * CHUNK >> level) // BLOCK
                if level >= 2:
                    key_block = own - 1 + 2 * (key // BLOCK)
                    allowed = key >= 0
                else:
                    key_block = own - 1 + key // BLOCK
                    distance = jnp.abs(key_block - own - (token >> level) // BLOCK)
                    allowed = distance <= 1 if level == 0 else distance == 1
                whole = place * per_run + key_block
                allowed = allowed & (whole >= 0) & (whole < per_run * sz.seq)
            mask_ref[i, pl.ds(sz.start[level], sz.keys[level])] = jnp.where(allowed, level * LN2, NEG)


def key_slices(sz, i, level):
    if level == TOP:
        return [(sz.offset[TOP], sz.top_keys)]
    if level < 2:
        return [(sz.offset[level] + (CHUNK >> level) * i, sz.keys[level])]
    own = (i * CHUNK) // (BLOCK << level)
    return [(sz.offset[level] + BLOCK * own, BLOCK), (sz.offset[level] + BLOCK * (own + 2), BLOCK)]


def take(ref, r, pieces, lanes):
    parts = [ref[r, pl.ds(pl.multiple_of(at, BLOCK) if not isinstance(at, int) else at, size), lanes] for at, size in pieces]
    return parts[0] if len(parts) == 1 else jnp.concatenate(parts, axis=0)


def give(ref, r, pieces, lanes, value):
    done = 0
    for at, size in pieces:
        rows = pl.ds(pl.multiple_of(at, BLOCK) if not isinstance(at, int) else at, size)
        ref[r, rows, lanes] += value[done : done + size]
        done += size


def two_heads(block):
    first = lax.broadcasted_iota(jnp.int32, block.shape, 1) < HDIM
    zero = jnp.zeros_like(block)
    return jnp.concatenate([jnp.where(first, block, zero), jnp.where(first, zero, block)], axis=0)


def one_row(block):
    first = lax.broadcasted_iota(jnp.int32, (CHUNK, 128), 1) < HDIM
    return jnp.where(first, block[:CHUNK], block[CHUNK:])


def chunk_queries(sz, q_ref, spread, r, i):
    tokens = pl.ds(pl.multiple_of(i * CHUNK, CHUNK), CHUNK)
    fine = q_ref[r, tokens, :]
    coarse = dot_nn(spread, fine).astype(BF16)
    return [fine] + [coarse[level * CHUNK : (level + 1) * CHUNK] for level in range(TOP)]


def attend(sz, q_ref, key_ref, value_ref, mask_ref, att_ref, lse_ref):
    spread = spread_matrix()

    def chunk(step, carry):
        r, i = step // sz.chunks, step % sz.chunks
        tokens = pl.ds(pl.multiple_of(i * CHUNK, CHUNK), CHUNK)
        queries = chunk_queries(sz, q_ref, spread, r, i)
        for pair in range(sz.pairs):
            lanes = slice(128 * pair, 128 * pair + 128)
            scores, values = [], []
            for level in range(LEVELS):
                pieces = key_slices(sz, i, level)
                keys = take(key_ref, r, pieces, lanes)
                values.append(take(value_ref, r, pieces, lanes))
                scores.append(dot_nt(keys, two_heads(queries[level][:, lanes])))
            scores = jnp.concatenate(scores, axis=0) + mask_ref[i]
            peak = jnp.max(scores, axis=0, keepdims=True)
            weights = jnp.exp(scores - peak)
            total = jnp.sum(weights, axis=0, keepdims=True)
            weights = (weights * (1.0 / total)).astype(BF16)
            mixed = dot_tn(weights, jnp.concatenate(values, axis=0))
            att_ref[r, tokens, lanes] = one_row(mixed).astype(BF16)
            lse_ref[step, pair : pair + 1, :] = peak + jnp.log(total)
        return carry

    lax.fori_loop(0, sz.rows * sz.chunks, chunk, 0)


def attend_back(sz, q_ref, key_ref, value_ref, mask_ref, lse_ref, go_ref, dq_ref, dkey_ref, dvalue_ref):
    spread = spread_matrix()
    dkey_ref[...] = jnp.zeros_like(dkey_ref)
    dvalue_ref[...] = jnp.zeros_like(dvalue_ref)

    def chunk(step, carry):
        r, i = step // sz.chunks, step % sz.chunks
        tokens = pl.ds(pl.multiple_of(i * CHUNK, CHUNK), CHUNK)
        queries = chunk_queries(sz, q_ref, spread, r, i)
        for pair in range(sz.pairs):
            lanes = slice(128 * pair, 128 * pair + 128)
            pieces = [key_slices(sz, i, level) for level in range(LEVELS)]
            keys = [take(key_ref, r, piece, lanes) for piece in pieces]
            values = jnp.concatenate([take(value_ref, r, piece, lanes) for piece in pieces], axis=0)
            doubled = [two_heads(level_queries[:, lanes]) for level_queries in queries]
            scores = jnp.concatenate([dot_nt(k, q) for k, q in zip(keys, doubled)], axis=0) + mask_ref[i]
            weights = jnp.exp(scores - lse_ref[step, pair : pair + 1, :])
            go = two_heads(go_ref[r, tokens, lanes])
            dweights = dot_nt(values, go)
            inner = jnp.sum(weights * dweights, axis=0, keepdims=True)
            dscores = (weights * (dweights - inner)).astype(BF16)
            dvalues = dot_nn(weights.astype(BF16), go)
            fine, coarse = None, []
            for level in range(LEVELS):
                part = slice(sz.start[level], sz.start[level] + sz.keys[level])
                give(dvalue_ref, r, pieces[level], lanes, dvalues[part])
                give(dkey_ref, r, pieces[level], lanes, dot_nn(dscores[part], doubled[level]))
                dquery = one_row(dot_tn(dscores[part], keys[level]))
                if level == 0:
                    fine = dquery
                else:
                    coarse.append(dquery.astype(BF16))
            fine = fine + dot_tn(spread, jnp.concatenate(coarse, axis=0))
            dq_ref[r, tokens, lanes] = (fine * HDIM**-0.5).astype(BF16)
        return carry

    lax.fori_loop(0, sz.rows * sz.chunks, chunk, 0)


def rim_rows(r, level, kind):
    return pl.ds(((r * TOP + level) * 2 + kind) * BLOCK, BLOCK)


def unpack_small(sz, small, vec_ref, up_ref):
    lane = lax.broadcasted_iota(jnp.int32, (BLOCK, 128), 1)
    tiles = [small[BLOCK * i : BLOCK * i + BLOCK, :].astype(F32) for i in range(sz.model // BLOCK)]
    for c in range(sz.model // 128):
        total = tiles[8 * c]
        for j in range(1, 8):
            total = jnp.where(lane // 16 == j, tiles[8 * c + j], total)
        vec_ref[:, 128 * c : 128 * c + 128] = total[:8]
    wide = sz.hidden * BLOCK // sz.model
    for c in range(sz.hidden // 128):
        total = tiles[2 * c]
        total = jnp.where(lane >= wide, tiles[2 * c + 1], total)
        up_ref[:, 128 * c : 128 * c + 128] = total[8:9]


def before_kernel(sz, x_ref, w_ref, q_ref, key_ref, value_ref, rims_ref, top_ref, vec_ref, up_ref):
    model = sz.model
    unpack_small(sz, w_ref[:, 8 * model : 8 * model + 128], vec_ref, up_ref)
    coarse = coarse_matrix(sz.run)
    for r in range(sz.rows):
        hat, _ = normalise(x_ref[pl.ds(r * sz.run, sz.run), :])
        normed = (hat * vec_ref[0:1, :] + vec_ref[2:3, :]).astype(BF16)
        queries = (dot_nn(normed, w_ref[:, :model]) + vec_ref[3:4, :]).astype(BF16)
        q_ref[r] = queries * jnp.asarray(HDIM**-0.5, BF16)
        for kind, bank in ((0, key_ref), (1, value_ref)):
            mixed = dot_nn(normed, w_ref[:, (1 + kind) * model : (2 + kind) * model])
            if kind == 1:
                mixed = mixed + vec_ref[4:5, :]
            mixed = mixed.astype(BF16)
            levels = dot_nn(coarse, mixed).astype(BF16)
            base = 0
            for level in range(LEVELS):
                n = sz.count[level]
                if level == 0:
                    now = mixed
                else:
                    now = levels[base : base + n]
                    base += n
                if level < TOP:
                    bank[r, pl.ds(sz.offset[level] + BLOCK, n), :] = now
                    rims_ref[0, rim_rows(r, level, kind), :] = now[n - BLOCK :]
                    rims_ref[1, rim_rows(r, level, kind), :] = now[:BLOCK]
                    bank[r, pl.ds(sz.offset[level], BLOCK), :] = jnp.zeros((BLOCK, model), BF16)
                    bank[r, pl.ds(sz.offset[level] + BLOCK + n, BLOCK), :] = jnp.zeros((BLOCK, model), BF16)
                else:
                    if kind == 0:
                        top_now = now
                    else:
                        top_ref[r] = jnp.concatenate([top_now, now], axis=0)


def place_rims(sz, low_ref, high_ref, tops_ref, key_ref, value_ref):
    for r in range(sz.rows):
        for kind, bank in ((0, key_ref), (1, value_ref)):
            for level in range(TOP):
                bank[r, pl.ds(sz.offset[level], BLOCK), :] = low_ref[rim_rows(r, level, kind), :]
                bank[r, pl.ds(sz.offset[level] + BLOCK + sz.count[level], BLOCK), :] = high_ref[rim_rows(r, level, kind), :]
            n = sz.count[TOP]
            for s in range(0, sz.seq, 2):
                both = jnp.concatenate(
                    [tops_ref[s, r, kind * n : kind * n + n, :], tops_ref[s + 1, r, kind * n : kind * n + n, :]], axis=0
                )
                bank[r, pl.ds(sz.offset[TOP] + s * n, 2 * n), :] = both


def after_kernel(
    sz, x_ref, q_ref, key_in, value_in, low_ref, high_ref, tops_ref, w_ref, down_ref, vec_ref, up_ref,
    att_ref, lse_ref, middle_ref, out_ref, key_ref, value_ref, mask_ref, second_ref,
):
    model = sz.model
    key_ref[...] = key_in[...]
    value_ref[...] = value_in[...]
    place_rims(sz, low_ref, high_ref, tops_ref, key_ref, value_ref)
    fill_mask(sz, mask_ref)
    attend(sz, q_ref, key_ref, value_ref, mask_ref, att_ref, lse_ref)
    for r in range(sz.rows):
        rows = pl.ds(r * sz.run, sz.run)
        middle = x_ref[rows, :] + dot_nn(att_ref[r], w_ref[:, 3 * model : 4 * model]) + vec_ref[5:6, :]
        middle_ref[rows, :] = middle
        hat, _ = normalise(middle)
        second_ref[rows, :] = (hat * vec_ref[1:2, :] + vec_ref[6:7, :]).astype(BF16)
        out_ref[rows, :] = middle + vec_ref[7:8, :]

    def part(c, carry):
        cols = pl.ds(pl.multiple_of(4 * model + c * model, 128), model)
        units = pl.ds(pl.multiple_of(c * model, 128), model)
        for r in range(sz.rows):
            rows = pl.ds(r * sz.run, sz.run)
            hidden = dot_nn(second_ref[rows, :], w_ref[:, cols]) + up_ref[:, units]
            out_ref[rows, :] += dot_nn(gelu(hidden).astype(BF16), down_ref[units, :])
        return carry

    lax.fori_loop(0, sz.hidden // model, part, 0)


def back_kernel(
    sz, g_ref, middle_ref, att_ref, q_ref, key_ref, value_ref, lse_ref, w_ref, down_ref, vec_ref, up_ref,
    dq_ref, dkey_ref, dvalue_ref, gm_ref, gout_ref, gup_ref, gdown_ref, gvec_ref, gupb_ref, rims_ref, tops_ref,
    mask_ref, second_ref, gd_ref, gs_ref, go_ref,
):
    model = sz.model
    fill_mask(sz, mask_ref)
    gvec_ref[...] = jnp.zeros_like(gvec_ref)
    for r in range(sz.rows):
        rows = pl.ds(r * sz.run, sz.run)
        hat, _ = normalise(middle_ref[rows, :])
        second_ref[rows, :] = (hat * vec_ref[1:2, :] + vec_ref[6:7, :]).astype(BF16)
        grad = g_ref[rows, :].astype(BF16)
        gd_ref[rows, :] = grad
        gvec_ref[7:8, :] += jnp.sum(grad.astype(F32), axis=0, keepdims=True)
        gs_ref[rows, :] = jnp.zeros((sz.run, model), F32)

    def part(c, carry):
        cols = pl.ds(pl.multiple_of(4 * model + c * model, 128), model)
        units = pl.ds(pl.multiple_of(c * model, 128), model)
        hidden = dot_nn(second_ref[...], w_ref[:, cols]) + up_ref[:, units]
        active, slope = gelu_both(hidden)
        gdown_ref[units, :] = dot_tn(active.astype(BF16), gd_ref[...]).astype(BF16)
        grad_hidden = (slope * dot_nt(gd_ref[...], down_ref[units, :])).astype(BF16)
        gupb_ref[:, units] = jnp.sum(grad_hidden.astype(F32), axis=0, keepdims=True)
        gup_ref[:, units] = dot_tn(second_ref[...], grad_hidden).astype(BF16)
        gs_ref[...] += dot_nt(grad_hidden, w_ref[:, cols])
        return carry

    lax.fori_loop(0, sz.hidden // model, part, 0)
    for r in range(sz.rows):
        rows = pl.ds(r * sz.run, sz.run)
        hat, inverse = normalise(middle_ref[rows, :])
        grad = gs_ref[rows, :]
        gvec_ref[1:2, :] += jnp.sum(grad * hat, axis=0, keepdims=True)
        gvec_ref[6:7, :] += jnp.sum(grad, axis=0, keepdims=True)
        gm = g_ref[rows, :] + norm_back(grad, hat, inverse, vec_ref[1:2, :])
        gm_ref[rows, :] = gm
        branch = gm.astype(BF16)
        gd_ref[rows, :] = branch
        gvec_ref[5:6, :] += jnp.sum(branch.astype(F32), axis=0, keepdims=True)
        go_ref[r] = dot_nt(branch, w_ref[:, 3 * model : 4 * model]).astype(BF16)
    gout_ref[...] = sum(
        dot_tn(att_ref[r], gd_ref[pl.ds(r * sz.run, sz.run), :]) for r in range(sz.rows)
    ).astype(BF16)
    attend_back(sz, q_ref, key_ref, value_ref, mask_ref, lse_ref, go_ref, dq_ref, dkey_ref, dvalue_ref)
    n = sz.count[TOP]
    for r in range(sz.rows):
        for kind, bank in ((0, dkey_ref), (1, dvalue_ref)):
            for level in range(TOP):
                rims_ref[0, rim_rows(r, level, kind), :] = bank[r, pl.ds(sz.offset[level], BLOCK), :].astype(BF16)
                rims_ref[1, rim_rows(r, level, kind), :] = bank[
                    r, pl.ds(sz.offset[level] + BLOCK + sz.count[level], BLOCK), :
                ].astype(BF16)
        for s in range(sz.seq):
            at = pl.ds(sz.offset[TOP] + s * n, n)
            tops_ref[s, r] = jnp.concatenate([dkey_ref[r, at, :], dvalue_ref[r, at, :]], axis=0).astype(BF16)


def last_kernel(
    sz, x_ref, gm_ref, dq_ref, dkey_ref, dvalue_ref, low_ref, high_ref, tops_ref, w_ref, vec_ref, gvec_in, gupb_ref,
    gin_ref, gqkv_ref, small_ref, gvec_ref, dk_ref, dv_ref, levels_ref, normed_ref,
):
    model = sz.model
    coarse = coarse_matrix(sz.run)
    gvec_ref[...] = gvec_in[...]
    for r in range(sz.rows):
        for kind, bank, out in ((0, dkey_ref, dk_ref), (1, dvalue_ref, dv_ref)):
            base = 0
            for level in range(LEVELS):
                n = sz.count[level]
                if level == TOP:
                    levels_ref[pl.ds(base, 2 * n), :] = jnp.concatenate(
                        [
                            sum(tops_ref[s, r, kind * n : kind * n + n, :].astype(F32) for s in range(sz.seq)),
                            jnp.zeros((n, model), F32),
                        ],
                        axis=0,
                    ).astype(BF16)
                    continue
                own = bank[r, pl.ds(sz.offset[level] + BLOCK, n), :]
                first = high_ref[rim_rows(r, level, kind), :].astype(F32)
                final = low_ref[rim_rows(r, level, kind), :].astype(F32)
                if n == BLOCK:
                    own = own + first + final
                else:
                    middle = [own[BLOCK : n - BLOCK]] if n > 2 * BLOCK else []
                    own = jnp.concatenate([own[:BLOCK] + first, *middle, own[n - BLOCK :] + final], axis=0)
                if level == 0:
                    fine = own
                else:
                    levels_ref[pl.ds(base, n), :] = own.astype(BF16)
                    base += n
            out[pl.ds(r * sz.run, sz.run), :] = (fine + dot_tn(coarse, levels_ref[...])).astype(BF16)
    for r in range(sz.rows):
        rows = pl.ds(r * sz.run, sz.run)
        gvec_ref[3:4, :] += jnp.sum(dq_ref[r].astype(F32), axis=0, keepdims=True)
        gvec_ref[4:5, :] += jnp.sum(dv_ref[rows, :].astype(F32), axis=0, keepdims=True)
        grad = dot_nt(dq_ref[r], w_ref[:, :model])
        grad = grad + dot_nt(dk_ref[rows, :], w_ref[:, model : 2 * model])
        grad = grad + dot_nt(dv_ref[rows, :], w_ref[:, 2 * model : 3 * model])
        hat, inverse = normalise(x_ref[rows, :])
        normed_ref[r] = (hat * vec_ref[0:1, :] + vec_ref[2:3, :]).astype(BF16)
        gvec_ref[0:1, :] += jnp.sum(grad * hat, axis=0, keepdims=True)
        gvec_ref[2:3, :] += jnp.sum(grad, axis=0, keepdims=True)
        gin_ref[rows, :] = gm_ref[rows, :] + norm_back(grad, hat, inverse, vec_ref[0:1, :])
    run = sz.run
    gqkv_ref[:, :model] = sum(dot_tn(normed_ref[r], dq_ref[r]) for r in range(sz.rows)).astype(BF16)
    gqkv_ref[:, model : 2 * model] = sum(
        dot_tn(normed_ref[r], dk_ref[pl.ds(r * run, run), :]) for r in range(sz.rows)
    ).astype(BF16)
    gqkv_ref[:, 2 * model :] = sum(
        dot_tn(normed_ref[r], dv_ref[pl.ds(r * run, run), :]) for r in range(sz.rows)
    ).astype(BF16)
    for i in range(model // BLOCK):
        top = gvec_ref[:, 128 * (i // 8) : 128 * (i // 8) + 128]
        up = jnp.broadcast_to(gupb_ref[:, 128 * (i // 2) : 128 * (i // 2) + 128], (8, 128))
        small_ref[pl.ds(BLOCK * i, BLOCK), :] = jnp.concatenate([top, up], axis=0).astype(BF16)


def call(kernel, name, outs, scratch, *args):
    whole = pl.BlockSpec(memory_space=pltpu.VMEM)
    return pl.pallas_call(
        kernel,
        out_shape=[jax.ShapeDtypeStruct(shape, dtype) for shape, dtype in outs],
        in_specs=[whole] * len(args),
        out_specs=[whole] * len(outs),
        scratch_shapes=[pltpu.VMEM(shape, dtype) for shape, dtype in scratch],
        compiler_params=pltpu.CompilerParams(vmem_limit_bytes=VMEM_LIMIT),
        name=name,
    )(*args)


def layer_before(sz, x, w):
    n, bank = sz.model, (sz.rows, sz.bank, sz.model)
    return call(
        functools.partial(before_kernel, sz),
        "before",
        [
            ((sz.rows, sz.run, n), BF16), (bank, BF16), (bank, BF16), ((2, sz.rim, n), BF16),
            ((sz.rows, BLOCK, n), BF16), ((8, n), F32), ((1, sz.hidden), F32),
        ],
        [],
        x, w,
    )


def layer_after(sz, x, q, keys, values, low, high, tops, w, down, vec, up):
    n, bank = sz.model, (sz.rows, sz.bank, sz.model)
    return call(
        functools.partial(after_kernel, sz),
        "after",
        [
            ((sz.rows, sz.run, n), BF16), ((sz.rows * sz.chunks, sz.pairs, 128), F32), ((sz.tokens, n), F32),
            ((sz.tokens, n), F32), (bank, BF16), (bank, BF16),
        ],
        [((sz.chunks, sz.width, 128), F32), ((sz.tokens, n), BF16)],
        x, q, keys, values, low, high, tops, w, down, vec, up,
    )


def layer_back(sz, g, middle, att, q, keys, values, lse, w, down, vec, up):
    n, bank = sz.model, (sz.rows, sz.bank, sz.model)
    return call(
        functools.partial(back_kernel, sz),
        "back",
        [
            ((sz.rows, sz.run, n), BF16), (bank, F32), (bank, F32), ((sz.tokens, n), F32), ((n, n), BF16),
            ((n, sz.hidden), BF16), ((sz.hidden, n), BF16), ((8, n), F32), ((1, sz.hidden), F32),
            ((2, sz.rim, n), BF16), ((sz.seq, sz.rows, BLOCK, n), BF16),
        ],
        [
            ((sz.chunks, sz.width, 128), F32), ((sz.tokens, n), BF16), ((sz.tokens, n), BF16), ((sz.tokens, n), F32),
            ((sz.rows, sz.run, n), BF16),
        ],
        g, middle, att, q, keys, values, lse, w, down, vec, up,
    )


def layer_last(sz, x, gm, dq, dkeys, dvalues, low, high, tops, w, vec, gvec, gupb):
    n = sz.model
    return call(
        functools.partial(last_kernel, sz),
        "last",
        [((sz.tokens, n), F32), ((n, 3 * n), BF16), ((n, 128), BF16)],
        [
            ((8, n), F32), ((sz.tokens, n), BF16), ((sz.tokens, n), BF16), ((sz.run, n), BF16),
            ((sz.rows, sz.run, n), BF16),
        ],
        x, gm, dq, dkeys, dvalues, low, high, tops, w, vec, gvec, gupb,
    )


MESH = pl.DeviceIdType.MESH
ORDERS = ("zyx", "zxy", "zxy", "zyx")


class Grid:
    def __init__(self, depth):
        dp, seq = lax.axis_index("dp"), lax.axis_index("seq")
        self.depth = depth
        self.z, self.x, self.y, self.c = dp // 2, dp % 2, seq // 2, seq % 2

    def at(self, z, x, y, c):
        return (z * 2 + x, y * 2 + c)

    def index(self, z, x, y, c):
        return z * 8 + x * 4 + y * 2 + c

    def partner(self, axis):
        z, x, y, c = self.z, self.x, self.y, self.c
        return self.at(z, 1 - x if axis == "x" else x, 1 - y if axis == "y" else y, 1 - c if axis == "c" else c)

    def up(self, by):
        return self.at(self.z + by, self.x, self.y, self.c)


def greet(devices):
    barrier = pltpu.get_barrier_semaphore()
    peers = jnp.int32(0)
    for where, condition in devices:
        signal = functools.partial(pl.semaphore_signal, barrier, inc=1, device_id=where, device_id_type=MESH)
        if condition is None:
            signal()
            peers += 1
        else:
            pl.when(condition)(signal)
            peers += condition.astype(jnp.int32)
    pl.semaphore_wait(barrier, peers)


def both(first, second):
    if first is None:
        return second
    return first if second is None else first & second


def when(condition, act):
    if condition is None:
        act()
    else:
        pl.when(condition)(act)


def gather_kernel(depth, big_ref, down_ref, big_out, down_out, local_sem, send_sem, recv_sem):
    grid = Grid(depth)
    z, x, y, c = grid.z, grid.x, grid.y, grid.c
    greet(
        [(grid.partner(axis), None) for axis in "cxy"] + [(grid.up(1), z + 1 < depth), (grid.up(-1), z > 0)]
    )
    pieces = []
    for layer in range(LAYERS):
        pieces.append((big_ref.at[layer], big_out.at[layer], big_ref.shape[1]))
        pieces.append((down_ref.at[layer], down_out.at[layer], down_ref.shape[1]))
    me = grid.index(z, x, y, c)
    sends, used = [], [0] * len(pieces)

    def copy(p, source, block, slot, to):
        _, out, rows = pieces[p]
        target = out.at[pl.ds(pl.multiple_of(block * rows, BLOCK), rows)]
        return pltpu.make_async_remote_copy(
            src_ref=target if source is None else source,
            dst_ref=target,
            send_sem=send_sem.at[p, slot],
            recv_sem=recv_sem.at[p, block],
            device_id=to,
            device_id_type=MESH,
        )

    def local(p):
        source, out, rows = pieces[p]
        return pltpu.make_async_copy(
            source, out.at[pl.ds(pl.multiple_of(me * rows, BLOCK), rows)], local_sem.at[p]
        )

    def send(p, source, block, to, condition):
        slot = used[p]
        used[p] += 1
        when(condition, lambda: copy(p, source, block, slot, to).start())
        sends.append((p, block, slot, to, condition))

    def receive(p, block, condition):
        when(condition, lambda: copy(p, None, block, 0, grid.partner("c")).wait_recv())

    def pass_on(p, source, block, axes, condition):
        for axis in axes:
            if axis == "z":
                send(p, source, block, grid.up(1), both(condition, z + 1 < depth))
                send(p, source, block, grid.up(-1), both(condition, z > 0))
            else:
                send(p, source, block, grid.partner(axis), condition)

    def start(p):
        local(p).start()
        pass_on(p, pieces[p][0], me, ORDERS[p % len(ORDERS)] + "c", None)

    def arrive(p, dz, sign, dx, dy):
        order = ORDERS[p % len(ORDERS)]
        from_z = z - sign * dz
        valid = (from_z >= 0) & (from_z < depth) if dz else None
        block = grid.index(from_z, 1 - x if dx else x, 1 - y if dy else y, c)
        receive(p, block, valid)
        away = {"z": dz, "x": dx, "y": dy}
        final = max(j for j, axis in enumerate(order) if away[axis])
        if order[final] == "z" and dz < depth - 1:
            onward = z + sign
            send(p, None, block, grid.up(sign), both(valid, (onward >= 0) & (onward < depth)))
        pass_on(p, None, block, order[final + 1 :] + "c", valid)

    for p in range(len(pieces)):
        start(p)
    events = []
    for p in range(len(pieces)):
        for dx in range(2):
            for dy in range(2):
                for dz in range(depth):
                    for sign in (1, -1) if dz else (1,):
                        if dx + dy + dz:
                            events.append((dx + dy + dz, p, dz, sign, dx, dy))
    for _, p, dz, sign, dx, dy in sorted(events, key=lambda event: event[:2]):
        arrive(p, dz, sign, dx, dy)
    for p in range(len(pieces)):
        local(p).wait()
        for zz in range(depth):
            for xx in range(2):
                for yy in range(2):
                    receive(p, grid.index(zz, xx, yy, 1 - c), None)
    for p, block, slot, to, condition in sends:
        when(condition, lambda: copy(p, None, block, slot, to).wait_send())


def scatter_kernel(depth, *refs):
    count = (len(refs) - 2) // 7
    pieces, sums = refs[:count], refs[count : 2 * count]
    buffers = [refs[2 * count + 5 * p : 2 * count + 5 * p + 5] for p in range(count)]
    send_sem, recv_sem = refs[-2], refs[-1]
    grid = Grid(depth)
    z, x, y, c = grid.z, grid.x, grid.y, grid.c
    others = [lax.rem(z + k, depth) for k in range(1, depth)]
    greet([(grid.partner(axis), None) for axis in "cxy"] + [(grid.at(other, x, y, c), None) for other in others])
    sends = []

    def move(p, stage, source, target, to):
        return pltpu.make_async_remote_copy(
            src_ref=source, dst_ref=target, send_sem=send_sem.at[p, stage], recv_sem=recv_sem.at[p, stage],
            device_id=to, device_id_type=MESH,
        )

    def first(p, stage):
        copy = move(p, stage, pieces[p].at[:, :, :, 1 - c], buffers[p][0], grid.partner("c"))
        copy.start()
        sends.append(copy)

    def swap(p, stage):
        piece, (from_core, from_first, from_second, held, _) = pieces[p], buffers[p]
        sends[p + (stage - 1) * count].wait_recv()
        axis = ("xy", "yx")[p % 2][stage - 1]
        lead = ("xy", "yx")[p % 2][0]
        if stage == 1:
            for zz in range(depth):
                for xx in range(2):
                    for yy in range(2):
                        total = piece[zz, xx, yy, c].astype(F32) + from_core[zz, xx, yy].astype(F32)
                        from_core[zz, xx, yy] = total.astype(BF16)
            source = from_core.at[:, 1 - x] if axis == "x" else from_core.at[:, :, 1 - y]
            copy = move(p, stage, source, from_first, grid.partner(axis))
        else:
            for zz in range(depth):
                for k in range(2):
                    kept = from_core[zz, x, k] if lead == "x" else from_core[zz, k, y]
                    from_first[zz, k] = (kept.astype(F32) + from_first[zz, k].astype(F32)).astype(BF16)
            other = 1 - (x if axis == "x" else y)
            copy = move(p, stage, from_first.at[:, other], from_second, grid.partner(axis))
        copy.start()
        sends.append(copy)

    def along(p):
        _, from_first, from_second, held, from_z = buffers[p]
        sends[p + 2 * count].wait_recv()
        mine = (y, x)[p % 2]
        for zz in range(depth):
            held[zz] = (from_first[zz, mine].astype(F32) + from_second[zz].astype(F32)).astype(BF16)
        for k, other in enumerate(others):
            copy = move(p, 3 + k, held.at[other], from_z.at[k], grid.at(other, x, y, c))
            copy.start()
            sends.append(copy)

    def finish(p):
        held, from_z = buffers[p][3], buffers[p][4]
        total = held[z].astype(F32)
        for k in range(depth - 1):
            sends[3 * count + p * (depth - 1) + k].wait_recv()
            total = total + from_z[k].astype(F32)
        sums[p][...] = total

    for p in range(count):
        first(p, 0)
    for p in range(count):
        swap(p, 1)
    for p in range(count):
        swap(p, 2)
    for p in range(count):
        along(p)
    for p in range(count):
        finish(p)
    for copy in sends:
        copy.wait_send()


def rim_kernel(seq, to_next_ref, to_last_ref, tops_ref, low_ref, high_ref, all_ref, send_sem, recv_sem):
    me, dp = lax.axis_index("seq"), lax.axis_index("dp")
    others = [lax.rem(me + k, seq) for k in range(1, seq)]
    greet([((dp, other), None) for other in others])
    ahead = pltpu.make_async_remote_copy(
        src_ref=to_next_ref, dst_ref=low_ref, send_sem=send_sem.at[0], recv_sem=recv_sem.at[0],
        device_id=(dp, me + 1), device_id_type=MESH,
    )
    behind = pltpu.make_async_remote_copy(
        src_ref=to_last_ref, dst_ref=high_ref, send_sem=send_sem.at[1], recv_sem=recv_sem.at[1],
        device_id=(dp, me - 1), device_id_type=MESH,
    )
    when(me + 1 < seq, ahead.start)
    when(me > 0, behind.start)
    tops = []
    for k, other in enumerate(others):
        source = tops_ref.at[0] if tops_ref.shape[0] == 1 else tops_ref.at[other]
        tops.append(
            pltpu.make_async_remote_copy(
                src_ref=source, dst_ref=all_ref.at[me], send_sem=send_sem.at[2 + k], recv_sem=recv_sem.at[2 + k],
                device_id=(dp, other), device_id_type=MESH,
            )
        )
        tops[-1].start()
    all_ref[me] = tops_ref[0] if tops_ref.shape[0] == 1 else tops_ref[me]

    @pl.when(me == 0)
    def _():
        low_ref[...] = jnp.zeros_like(low_ref)

    @pl.when(me == seq - 1)
    def _():
        high_ref[...] = jnp.zeros_like(high_ref)

    when(me > 0, ahead.wait_recv)
    when(me + 1 < seq, behind.wait_recv)
    for copy in tops:
        copy.wait_recv()
    when(me + 1 < seq, ahead.wait_send)
    when(me > 0, behind.wait_send)
    for copy in tops:
        copy.wait_send()


def exchange(sz, collective, to_next, to_last, tops):
    whole = pl.BlockSpec(memory_space=pltpu.VMEM)
    rim = jax.ShapeDtypeStruct(to_next.shape, BF16)
    return pl.pallas_call(
        functools.partial(rim_kernel, sz.seq),
        out_shape=[rim, rim, jax.ShapeDtypeStruct((sz.seq,) + tops.shape[1:], BF16)],
        in_specs=[whole] * 3,
        out_specs=[whole] * 3,
        scratch_shapes=[pltpu.SemaphoreType.DMA((sz.seq + 1,)), pltpu.SemaphoreType.DMA((sz.seq + 1,))],
        compiler_params=pltpu.CompilerParams(
            collective_id=collective, has_side_effects=True, vmem_limit_bytes=VMEM_LIMIT
        ),
        name=("rims", "rims_back")[collective - 1],
    )(to_next, to_last, tops)


def direct(rows):
    return lax.axis_size("seq") == 4 and lax.axis_size("dp") % 2 == 0 and rows % BLOCK == 0


def pack_small(gains, biases, up_bias):
    layers, _, features = gains.shape
    tiles = features // BLOCK
    vec = jnp.concatenate([gains, biases], axis=1).reshape(layers, 8, tiles, BLOCK).transpose(0, 2, 1, 3)
    vec = jnp.tile(vec, (1, 1, 1, 128 // BLOCK))
    up = up_bias.reshape(layers, tiles, 1, up_bias.shape[1] // tiles)
    up = jnp.broadcast_to(jnp.tile(up, (1, 1, 1, 128 // up.shape[3])), (layers, tiles, 8, 128))
    return jnp.concatenate([vec, up], axis=2).reshape(layers, features, 128)


def gather_weights(w_qkv, w_out, w_up, w_down, gains, biases, up_bias):
    whole = lambda array, axis: lax.all_gather(array, AXES, axis=axis, tiled=True)
    if not direct(w_qkv.shape[1]):
        big = whole(jnp.concatenate([w_qkv, w_out, w_up], axis=2), 1)
        small = pack_small(whole(gains, 2), whole(biases, 2), whole(up_bias, 1))
        return jnp.concatenate([big, small], axis=2), whole(w_down, 1)
    big = jnp.concatenate([w_qkv, w_out, w_up, pack_small(gains, biases, up_bias)], axis=2)
    depth = lax.axis_size("dp") // 2
    blocks = 8 * depth
    anywhere = pl.BlockSpec(memory_space=pl.ANY)
    outs = [
        jax.ShapeDtypeStruct((LAYERS, blocks * array.shape[1], array.shape[2]), BF16) for array in (big, w_down)
    ]
    return pl.pallas_call(
        functools.partial(gather_kernel, depth),
        out_shape=outs,
        in_specs=[anywhere] * 2,
        out_specs=[anywhere] * 2,
        scratch_shapes=[
            pltpu.SemaphoreType.DMA((2 * LAYERS,)),
            pltpu.SemaphoreType.DMA((2 * LAYERS, 16 * depth)),
            pltpu.SemaphoreType.DMA((2 * LAYERS, blocks)),
        ],
        compiler_params=pltpu.CompilerParams(collective_id=0, has_side_effects=True),
        name="gather",
    )(big, w_down)


def unpack_grads(sz, qkv, out, up, small, down):
    wide = sz.hidden * BLOCK // sz.model
    per = 128 // wide
    place = lax.axis_index("dp") * lax.axis_size("seq") + lax.axis_index("seq")
    vec = lax.dynamic_slice(small, (0, BLOCK * (place % 8)), (8, BLOCK))
    return qkv, out, up, down, vec[:2], vec[2:], lax.dynamic_slice(small, (8, wide * (place % per)), (1, wide))[0]


def scatter_grads(sz, layers):
    if direct(sz.model // (lax.axis_size("dp") * lax.axis_size("seq"))):
        depth = lax.axis_size("dp") // 2
        whole = pl.BlockSpec(memory_space=pltpu.VMEM)
        pieces = [
            array.reshape((depth, 2, 2, 2, array.shape[0] // (8 * depth), array.shape[1]))
            for parts in layers
            for array in parts
        ]
        outs, scratch = [], []
        for piece in pieces:
            block = piece.shape[4:]
            outs.append(jax.ShapeDtypeStruct(block, F32))
            for lead in ((depth, 2, 2), (depth, 2), (depth,), (depth,), (depth - 1,)):
                scratch.append(pltpu.VMEM(lead + block, BF16))
        stages = 2 + depth
        sums = pl.pallas_call(
            functools.partial(scatter_kernel, depth),
            out_shape=outs,
            in_specs=[whole] * len(pieces),
            out_specs=[whole] * len(pieces),
            scratch_shapes=scratch + [pltpu.SemaphoreType.DMA((len(pieces), stages))] * 2,
            compiler_params=pltpu.CompilerParams(
                collective_id=3, has_side_effects=True, vmem_limit_bytes=VMEM_LIMIT
            ),
            name="scatter",
        )(*pieces)
        per = len(sums) // LAYERS
        return [unpack_grads(sz, *sums[per * layer : per * layer + per]) for layer in range(LAYERS)]
    return [scatter_by_sums(sz, parts) for parts in layers]


def scatter_by_sums(sz, parts):
    gqkv, gout, gup, small, gdown = parts
    spread = lambda array, axis: lax.psum_scatter(
        array.astype(F32), AXES, scatter_dimension=axis, tiled=True
    )
    tiles = small.reshape(sz.model // BLOCK, BLOCK, 128)
    vec = jnp.concatenate(
        [tiles[i, :8, BLOCK * (i % 8) : BLOCK * (i % 8) + BLOCK] for i in range(sz.model // BLOCK)], axis=1
    )
    wide = sz.hidden * BLOCK // sz.model
    per = 128 // wide
    up = jnp.concatenate(
        [tiles[i, 8, wide * (i % per) : wide * (i % per) + wide] for i in range(sz.model // BLOCK)], axis=0
    )
    vec = spread(vec, 1)
    return spread(gqkv, 0), spread(gout, 0), spread(gup, 0), spread(gdown, 0), vec[:2], vec[2:], spread(up, 0)


def on_device(
    tokens_in, grad_output, prefix_len, w_qkv, w_out, w_up, w_down, norm_gains, bias_rows, up_bias
):
    micro, rows, run, model = tokens_in.shape
    hidden = w_up.shape[2]
    seq = lax.axis_size("seq")
    sz = Sizes(micro * rows, run, model, hidden, seq)
    big, down = gather_weights(w_qkv, w_out, w_up, w_down, norm_gains, bias_rows, up_bias)
    state = tokens_in.astype(F32).reshape(sz.tokens, model)
    kept = []
    for layer in range(LAYERS):
        q, keys, values, rims, top, vec, up = layer_before(sz, state, big[layer])
        low, high, tops = exchange(sz, 1, rims[0], rims[1], top[None])
        att, lse, middle, out, keys, values = layer_after(
            sz, state, q, keys, values, low, high, tops, big[layer], down[layer], vec, up
        )
        kept.append((state, q, keys, values, att, lse, middle, vec, up))
        state = out
    out_act = state.astype(BF16).reshape(tokens_in.shape)
    positions = lax.axis_index("seq") * run + jnp.arange(run, dtype=jnp.int32)
    keep = positions >= prefix_len[..., None]
    grad = jnp.where(keep[..., None], grad_output.astype(F32), 0.0).reshape(sz.tokens, model)
    grads = [None] * LAYERS
    for layer in reversed(range(LAYERS)):
        x, q, keys, values, att, lse, middle, vec, up = kept[layer]
        dq, dkeys, dvalues, gm, gout, gup, gdown, gvec, gupb, rims, tops = layer_back(
            sz, grad, middle, att, q, keys, values, lse, big[layer], down[layer], vec, up
        )
        high, low, tops = exchange(sz, 2, rims[1], rims[0], tops)
        grad, gqkv, small = layer_last(sz, x, gm, dq, dkeys, dvalues, low, high, tops, big[layer], vec, gvec, gupb)
        grads[layer] = (gqkv, gout, gup, small, gdown)
    grads = scatter_grads(sz, grads)
    stacked = [jnp.stack([grads[layer][k] for layer in range(LAYERS)], axis=0) for k in range(7)]
    return (out_act, grad.reshape(tokens_in.shape), *stacked)


def solution(mesh):
    tokens, shard = P(None, "dp", "seq", None), P(None, AXES, None)
    small, bias = P(None, None, AXES), P(None, AXES)
    return jax.shard_map(
        on_device,
        mesh=mesh,
        in_specs=(tokens, tokens, P(None, "dp"), shard, shard, shard, shard, small, small, bias),
        out_specs=(tokens, tokens, shard, shard, shard, shard, small, small, bias),
        check_vma=False,
    )
```

time: 3890 us -> 389 us (0.10)
  waiting for transfers between devices: 1460 us -> 0 us
  local copies, waits for them, and re-layouts: 1180 us -> 22 us
  other arithmetic: 423 us -> 16.2 us
  blocking collectives: 362 us -> 0 us
  matrix products: 355 us -> 0 us
  Pallas kernels: 0 us -> 349 us
    reduce_scatter x8 -> x0, waiting for transfers between devices: 1030 us -> none  [the longest x2 280 us: on_device(): lax.psum_scatter(grad_wdown, ('dp', 'seq'), scatter_dimension=0, tiled=True)]
    unnamed x38 -> x0, waiting for transfers between devices: 431 us -> none
    slice x404 -> x0, local copies, waits for them, and re-layouts: 357 us -> none  [the longest x120 178 us: coarsen(): return 0.5 * (field[:, 0::2] + field[:, 1::2])]
    dot_general x192 -> x0, matrix products: 355 us -> none  [the longest x20 47.1 us: attend_backward(): jnp.einsum('rbhij,rbihd->rbjhd', weigh_out[0].astype(jnp.bfloat16), grad_...]
    pallas_call x0 -> x14, Pallas kernels: none -> 349 us  [the longest x8 159 us: call(): pl.pallas_call(kernel, out_shape=[jax.ShapeDtypeStruct(shape, dtype) for...]
    all_gather x14 -> x0, blocking collectives: 280 us -> none  [the longest x2 80.8 us: fetch_layer(): lax.all_gather(w_out[layer_id], ('dp', 'seq'), axis=0, tiled=True)]
    broadcast_in_dim x424 -> x1, local copies, waits for them, and re-layouts: 257 us -> 0.01 us  [pack_small(): jnp.broadcast_to(jnp.tile(up, (1, 1, 1, 128 // up.shape[3])), (layers, ti...]
    unnamed x3007 -> x4, local copies, waits for them, and re-layouts: 175 us -> 1.28 us
where the time goes in v1:
time: 389 us; the launch traced here: 388 us
  Pallas kernels  349 us (90%)
  local copies, waits for them, and re-layouts  22 us (6%)
  other arithmetic  16.2 us (4%)
    pallas_call x8, Pallas kernels, call(): pl.pallas_call(kernel, out_shape=[jax.ShapeDtypeStruct(shape, dtype) for...  159 us
    pallas_call x1, Pallas kernels, scatter_grads(): pl.pallas_call(functools.partial(scatter_kernel, depth), out_shape=outs,...  88.8 us
    pallas_call x1, Pallas kernels, gather_weights(): pl.pallas_call(functools.partial(gather_kernel, depth), out_shape=outs, i...  62.5 us
    pallas_call x4, Pallas kernels, exchange(): pl.pallas_call(functools.partial(rim_kernel, sz.seq), out_shape=[rim, rim...  38.9 us

profile of v1, /device:TPU:0, one launch (start us, length us, event | category | flops | bytes accessed | tf_op | source)
XLA Modules:
  0.0 388.4 jit_solution(1171528739390174871)
XLA Ops:
  0.6 0.0 copy-start
  0.7 0.8 broadcast_compare_fusion
  1.5 0.7 copy.19
  2.2 0.7 tile.18
  2.8 0.1 tile.19
  2.9 0.7 pad_maximum_fusion.6
  3.6 0.1 tile.17
  3.7 1.7 pad_maximum_fusion.big_ref
  5.4 2.2 convert_select_fusion
  7.6 0.0 copy-done
  7.6 1.2 bitcast_convert_fusion.x_ref
  8.8 62.5 %gather.1 = (bf16[2,512,4224]{2,1,0:T(8,128)(2,1)}, bf16[2,2048,512]{2,1,0:T(8,128)(2,1)}) custom-call(bf16[2,16,4224]{2,1,0:T(8,128)(2,1)} %pad_maximum_fusion.big_ref, bf16[2,64,512]{2,1,0:T(8,128)(2,1)} %down_ref.1), custom_call_target="tpu_custom_call" | custom-call | tf_op jit(solution)/shard_map/gather/pallas_call | solution.py:845
  71.3 5.9 %slice_bitcast_fusion = (bf16[512,4224]{1,0:T(8,128)(2,1)}, bf16[512,4224]{1,0:T(8,128)(2,1)}) fusion(bf16[2,512,4224]{2,1,0:T(8,128)(2,1)} %get-tuple-element.87), kind=kLoop, calls=%fused_computation | loop fusion | bytes 17301504 | tf_op jit(solution)/shard_map/squeeze | solution.py:929
  77.3 6.2 %before.2 = (bf16[2,256,512]{2,1,0:T(8,128)(2,1)}, bf16[2,688,512]{2,1,0:T(8,128)(2,1)}, bf16[2,688,512]{2,1,0:T(8,128)(2,1)}, bf16[2,320,512]{2,1,0:T(8,128)(2,...) custom-call(f32[512,512]{1,0:T(8,128)} %bitcast_convert_fusion.x_ref, ...), custom_call_target="tpu_custom_call" | custom-call | tf_op jit(solution)/shard_map/before/pallas_call | solution.py:471
  83.4 1.9 slice_bitcast_fusion.10
  85.4 9.8 %rims.2 = (bf16[320,512]{1,0:T(8,128)(2,1)}, bf16[320,512]{1,0:T(8,128)(2,1)}, bf16[4,2,16,512]{3,2,1,0:T(8,128)(2,1)}) custom-call(bf16[320,512]{1,0:T(8,128)(2,1)} %get-tuple-element.185.to_next_ref, bf16[320,512]{1,0:T(8,128)(2,1)} %get-tuple-element.184.to_last_ref, bf16[1,2,16,512]{3,2,1,0:T(8,128)(2,1)} %bitcast.87), custom_call_target="tpu_custom_call" | custom-call | tf_op jit(solution)/shard_map/rims/pallas_call | solution.py:805
  95.2 4.5 %slice_bitcast_fusion.2 = (bf16[2048,512]{1,0:T(8,128)(2,1)}, bf16[2048,512]{1,0:T(8,128)(2,1)}) fusion(bf16[2,2048,512]{2,1,0:T(8,128)(2,1)} %get-tuple-element.96), kind=kLoop, calls=%fused_computation.2 | loop fusion | bytes 8388608 | tf_op jit(solution)/shard_map/squeeze | solution.py:932
  99.8 25.0 %after.2 = (bf16[2,256,512]{2,1,0:T(8,128)(2,1)}, f32[8,4,128]{2,1,0:T(4,128)}, f32[512,512]{1,0:T(8,128)}, f32[512,512]{1,0:T(8,128)}, bf16[2,688,512]{2,1,0:T(8,128)(2,1)}, /*index=5*/bf16[2,688,512]{2,1,0:T(8,128)(2,1)}) custom-call(f32[512,512]{1,0:T(8,128)} %bitcast_convert_fusion.x_ref, bf16[2,256,512]{2,1,0:T(8,128)(2,1)} %get-tuple-element.88.q_ref, ...), custom_call_target="tpu_custom_call" | custom-call | tf_op jit(solution)/shard_map/after/pallas_call | solution.py:471
  124.8 6.2 %before.3 = (bf16[2,256,512]{2,1,0:T(8,128)(2,1)}, bf16[2,688,512]{2,1,0:T(8,128)(2,1)}, bf16[2,688,512]{2,1,0:T(8,128)(2,1)}, bf16[2,320,512]{2,1,0:T(8,128)(2,...) custom-call(f32[512,512]{1,0:T(8,128)} %get-tuple-element.99.x_ref, ...), custom_call_target="tpu_custom_call" | custom-call | tf_op jit(solution)/shard_map/before/pallas_call | solution.py:471
  131.0 2.0 slice_bitcast_fusion.8
  133.0 9.7 %rims.3 = (bf16[320,512]{1,0:T(8,128)(2,1)}, bf16[320,512]{1,0:T(8,128)(2,1)}, bf16[4,2,16,512]{3,2,1,0:T(8,128)(2,1)}) custom-call(bf16[320,512]{1,0:T(8,128)(2,1)} %get-tuple-element.183.to_next_ref, bf16[320,512]{1,0:T(8,128)(2,1)} %get-tuple-element.182.to_last_ref, bf16[1,2,16,512]{3,2,1,0:T(8,128)(2,1)} %bitcast.88), custom_call_target="tpu_custom_call" | custom-call | tf_op jit(solution)/shard_map/rims/pallas_call | solution.py:805
  142.7 25.0 %after.3 = (bf16[2,256,512]{2,1,0:T(8,128)(2,1)}, f32[8,4,128]{2,1,0:T(4,128)}, f32[512,512]{1,0:T(8,128)}, f32[512,512]{1,0:T(8,128)}, bf16[2,688,512]{2,1,0:T(8,128)(2,1)}, /*index=5*/bf16[2,688,512]{2,1,0:T(8,128)(2,1)}) custom-call(f32[512,512]{1,0:T(8,128)} %get-tuple-element.99.x_ref, bf16[2,256,512]{2,1,0:T(8,128)(2,1)} %get-tuple-element.100.q_ref, ...), custom_call_target="tpu_custom_call" | custom-call | tf_op jit(solution)/shard_map/after/pallas_call | solution.py:471
  167.6 2.1 convert_element_type.7
  169.7 39.9 %back.2 = (bf16[2,256,512]{2,1,0:T(8,128)(2,1)}, f32[2,688,512]{2,1,0:T(8,128)}, f32[2,688,512]{2,1,0:T(8,128)}, f32[512,512]{1,0:T(8,128)}, bf16[512,512]{1,0:T...) custom-call(f32[512,512]{1,0:T(8,128)} %bitcast.67, ...), custom_call_target="tpu_custom_call" | custom-call | tf_op jit(solution)/shard_map/back/pallas_call | solution.py:471
  209.6 2.0 slice_bitcast_fusion.6
  211.6 9.7 %rims_back.2 = (bf16[320,512]{1,0:T(8,128)(2,1)}, bf16[320,512]{1,0:T(8,128)(2,1)}, bf16[4,2,16,512]{3,2,1,0:T(8,128)(2,1)}) custom-call(bf16[320,512]{1,0:T(8,128)(2,1)} %get-tuple-element.181.to_next_ref, bf16[320,512]{1,0:T(8,128)(2,1)} %get-tuple-element.180.to_last_ref, bf16[4,2,16,512]{3,2,1,0:T(8,128)(2,1)} %get-tuple-element.121.tops_ref), custom_call_target="tpu_custom_call" | custom-call | tf_op jit(solution)/shard_map/rims_back/pallas_call | solution.py:805
  221.3 8.5 %last.2 = (f32[512,512]{1,0:T(8,128)}, bf16[512,1536]{1,0:T(8,128)(2,1)}, bf16[512,128]{1,0:T(8,128)(2,1)}) custom-call(f32[512,512]{1,0:T(8,128)} %get-tuple-element.99.x_ref, f32[512,512]{1,0:T(8,128)} %get-tuple-element.116.gm_ref, bf16[2,256,512]{2,1,0:T(8,128)(2,1)} %get-tuple-element.117.dq_ref, f32[2,688,512]{2,1,0:T(8,128)} %get-tuple-element.118.dkey_ref, ...), custom_call_target="tpu_custom_call" | custom-call | tf_op jit(solution)/shard_map/last/pallas_call | solution.py:471
  229.8 39.9 %back.3 = (bf16[2,256,512]{2,1,0:T(8,128)(2,1)}, f32[2,688,512]{2,1,0:T(8,128)}, f32[2,688,512]{2,1,0:T(8,128)}, f32[512,512]{1,0:T(8,128)}, bf16[512,512]{1,0:T...) custom-call(f32[512,512]{1,0:T(8,128)} %get-tuple-element.127.g_ref,, ...), custom_call_target="tpu_custom_call" | custom-call | tf_op jit(solution)/shard_map/back/pallas_call | solution.py:471
  269.7 2.0 slice_bitcast_fusion.4
  271.7 9.7 %rims_back.3 = (bf16[320,512]{1,0:T(8,128)(2,1)}, bf16[320,512]{1,0:T(8,128)(2,1)}, bf16[4,2,16,512]{3,2,1,0:T(8,128)(2,1)}) custom-call(bf16[320,512]{1,0:T(8,128)(2,1)} %get-tuple-element.179.to_next_ref, bf16[320,512]{1,0:T(8,128)(2,1)} %get-tuple-element.178.to_last_ref, bf16[4,2,16,512]{3,2,1,0:T(8,128)(2,1)} %get-tuple-element.138.tops_ref), custom_call_target="tpu_custom_call" | custom-call | tf_op jit(solution)/shard_map/rims_back/pallas_call | solution.py:805
  281.4 8.5 %last.3 = (f32[512,512]{1,0:T(8,128)}, bf16[512,1536]{1,0:T(8,128)(2,1)}, bf16[512,128]{1,0:T(8,128)(2,1)}) custom-call(f32[512,512]{1,0:T(8,128)} %bitcast_convert_fusion.x_ref, f32[512,512]{1,0:T(8,128)} %get-tuple-element.133.gm_ref, bf16[2,256,512]{2,1,0:T(8,128)(2,1)} %get-tuple-element.134.dq_ref, f32[2,688,512]{2,1,0:T(8,128)} %get-tuple-element.135.dkey_ref, ...), custom_call_target="tpu_custom_call" | custom-call | tf_op jit(solution)/shard_map/last/pallas_call | solution.py:471
  289.9 88.8 %scatter.1 = (f32[16,1536]{1,0:T(8,128)}, f32[16,512]{1,0:T(8,128)}, f32[16,2048]{1,0:T(8,128)}, f32[16,128]{1,0:T(8,128)}, f32[64,512]{1,0:T(8,128)}, /*index=5...) custom-call(bf16[4,2,2,2,16,1536]{5,4,3,2,1,0:T(8,128)(2,1)} %bitcast.73, ...), custom_call_target="tpu_custom_call" | custom-call | tf_op jit(solution)/shard_map/scatter/pallas_call | solution.py:884
  378.7 1.6 pad_maximum_fusion.3
  380.4 0.8 constant_dynamic-slice_fusion
  381.1 0.8 constant_dynamic-slice_fusion.2
  381.9 0.6 pad_maximum_fusion.8
  382.5 0.6 copy.23
  383.1 0.6 pad_maximum_fusion.7
  383.7 1.4 pad_maximum_fusion.4
  385.1 1.7 pad_maximum_fusion.1
  386.7 1.7 pad_maximum_fusion.2
  (10 shorter events, 0.0 us)
Async XLA Ops:
  0.6 7.0 %copy-start = (bf16[2,1,256,512]{3,2,1,0:T(8,128)(2,1)S(1)}, bf16[2,1,256,512]{3,2,1,0:T(8,128)(2,1)}, u32[]{:S(2)}) copy-start(bf16[2,1,256,512]{3,2,1,0:T(8,128)(2,1)} %param.10) | copy-start | bytes 1572868
